TPU v7x, 32 devices: a whole 2x2x4 slice. The times are simulated.
32 devices in a mesh: sec: 2 (over x), shot: 8 (over z, core), win: 2 (over y).
Axes of the slice: x: 2, y: 2, z: 4, core: 2. Of those that a mesh axis runs over, the one named last changes fastest.
Arguments:
- shot_rows: bfloat16 [512, 4, 2, 4096], P('shot'), may hold values from -6 to 6
- aperture: int32 [512, 4], P('shot'), may hold values from 0 to 7, all different within a row; in each aligned block of 64 rows (0 to 63, 64 to 127, ...) at most 64 rows name the same one
- panel: bfloat16 [8, 2, 4096, 4096], P('shot', None, None, ('sec', 'win')), may hold values from -0.09375 to 0.09375
- recorded: bfloat16 [512, 2, 4096], P('shot', None, ('sec', 'win')), may hold values from -6 to 6
- shift: int32 [512], P('shot'), may hold values from 0 to 16
Outputs:
- predicted: float32 [512, 2, 4096], P('shot', None, ('sec', 'win'))
- primaries: float32 [512, 2, 4096], P('shot', None, ('sec', 'win'))
Inputs may be any that keep to these rules, and one draw needn't show every extreme that they name: `aperture`: each shot names 4 different panels. Among the 64 shots of one index of shot, no panel is named by more than 64 entries, a bound that some block reaches.
All inputs are finite; a program needn't handle non-finite values.
Results may differ from a plain program's by a relative error of at most 0.0003.
Values may be sent and summed in bfloat16 or wider, within the bound.
No kernel may reach another device: no remote copies, remote signals or barrier semaphores. Data moves between devices by JAX's collectives and lax.ppermute only.
A program may use at most 128 MiB of HBM per device.

v0:
```python
import jax
import jax.numpy as jnp
from jax import lax
from jax.sharding import PartitionSpec as P

TAPS = 31
WL = 256
LAG = 8


def extended(block, sides, width):
    for axis, dim in sides:
        count = lax.axis_size(axis)
        forward = [(i, i + 1) for i in range(count - 1)]
        backward = [(target, source) for source, target in forward]
        low = lax.ppermute(
            lax.slice_in_dim(block, block.shape[dim] - width, None, axis=dim), axis, forward
        )
        high = lax.ppermute(lax.slice_in_dim(block, 0, width, axis=dim), axis, backward)
        block = jnp.concatenate([low, block, high], axis=dim)
    return block


def complex_rows(rows_here, weights):
    parts = jnp.einsum("mck,dkr->mcdr", rows_here, weights, preferred_element_type=jnp.float32)
    real_part = parts[:, 0, 0] - parts[:, 1, 1]
    imag_part = parts[:, 0, 1] + parts[:, 1, 0]
    return jnp.stack([real_part, imag_part], axis=1)


def body(shot_rows, aperture, panel, recorded, shift):
    shot_count, slot_count = aperture.shape
    trace_width = shot_rows.shape[3]
    recv_width = panel.shape[3]
    row_count = shot_count * slot_count
    panel_count = lax.axis_size("shot")
    capacity = 2 * row_count // panel_count
    weights = panel[0]
    ap_flat = aperture.reshape(row_count)
    indicator = (ap_flat[:, None] == jnp.arange(panel_count, dtype=jnp.int32)[None, :]).astype(
        jnp.int32
    )
    earlier = jnp.cumsum(indicator, axis=0) - indicator
    position = jnp.sum(earlier * indicator, axis=1)
    slot_id = ap_flat * capacity + position
    source = (
        jnp.zeros((panel_count * capacity,), jnp.int32)
        .at[slot_id]
        .set(jnp.arange(row_count, dtype=jnp.int32))
    )
    filled = (
        jnp.zeros((panel_count * capacity,), jnp.bfloat16)
        .at[slot_id]
        .set(jnp.ones((row_count,), jnp.bfloat16))
    )
    rows_flat = shot_rows.reshape(row_count, 2, trace_width)
    outgoing = (rows_flat[source] * filled[:, None, None]).reshape(
        panel_count, capacity, 2, trace_width
    )
    received = lax.all_to_all(outgoing, "shot", split_axis=0, concat_axis=0, tiled=True)
    sources = received.shape[0]
    members = received.shape[1]
    stacked = received.reshape(sources * members, 2, trace_width)
    products = complex_rows(stacked, weights).reshape(sources, members, 2, recv_width)
    returned = lax.all_to_all(products, "shot", split_axis=0, concat_axis=0, tiled=True)
    back_flat = returned.reshape(panel_count * capacity, 2, recv_width)
    predicted = jnp.sum(back_flat[slot_id].reshape(shot_count, slot_count, 2, recv_width), axis=1)
    edge = (TAPS - 1) // 2 + LAG
    padded = extended(predicted, ((("sec", "win"), 2),), edge)
    span_width = recv_width + TAPS - 1

    def align_row(row, begin):
        return lax.dynamic_slice_in_dim(row, begin, span_width, 1)

    aligned = jax.vmap(align_row)(padded, shift)
    windows = recv_width // WL
    target = recorded.astype(jnp.float32).reshape(shot_count, 2, windows, WL)
    design = jnp.stack([aligned[:, :, tap : tap + recv_width] for tap in range(TAPS)], axis=2)
    design = design.reshape(shot_count, 2, TAPS, windows, WL)
    gram = jnp.einsum("scjwt,sckwt->swjk", design, design, precision=lax.Precision.HIGHEST)
    gram = gram + jnp.eye(TAPS, dtype=jnp.float32)
    moment = jnp.einsum("scjwt,scwt->swj", design, target, precision=lax.Precision.HIGHEST)
    factor = jnp.linalg.cholesky(gram)
    filters = jax.scipy.linalg.cho_solve((factor, True), moment[..., None])[..., 0]
    matched = jnp.einsum("swj,scjwt->scwt", filters, design, precision=lax.Precision.HIGHEST)
    primaries = (target - matched).reshape(shot_count, 2, recv_width)
    return (predicted, primaries)


def solution(mesh):
    in_specs = (
        P("shot", None, None, None),
        P("shot", None),
        P("shot", None, None, ("sec", "win")),
        P("shot", None, ("sec", "win")),
        P("shot"),
    )
    out_specs = (P("shot", None, ("sec", "win")), P("shot", None, ("sec", "win")))
    return jax.shard_map(body, mesh=mesh, in_specs=in_specs, out_specs=out_specs, check_vma=False)
```

profile of v0, /device:TPU:12, one launch (start us, length us, event | category | flops | bytes accessed | tf_op | source)
XLA Modules:
  0.0 1598.4 jit_solution(15374390568615959453)
XLA Ops:
  4.9 28.1 %gather_fusion = bf16[512,2,4096]{2,1,0:T(2,128)(2,1)} fusion(bf16[256,2,4096]{2,1,0:T(2,128)(2,1)} %bitcast.86, s32[1024]{0:T(1024)S(1)} %pad_clamp_fusion.1), kind=kCustom, calls=%fused_computation | custom fusion | bytes 16779264 | tf_op jit(solution)/shard_map/gather | solution.py:57
  33.0 12.6 copy.229
  48.1 7.4 broadcast_multiply_fusion
  55.6 7.7 copy.230
  63.3 187.9 %all_to_all.10 = bf16[8,64,2,4096]{3,1,2,0:T(8,128)(2,1)} all-to-all(bf16[8,64,2,4096]{3,1,2,0:T(8,128)(2,1)} %copy.230), channel_id=1, replica_groups=mesh['sec'=2,'shot'=8,'win'=2] {'shot'}, dimensions={0} | all-to-all | bytes 16777216 | tf_op jit(solution)/shard_map/all_to_all | solution.py:60
  251.2 7.7 copy.231
  258.9 21.5 %fusion = f32[512,2,2,1024]{3,0,2,1:T(8,128)S(1)} fusion(bf16[512,2,4096,1]{2,0,3,1:T(8,128)(2,1)} %bitcast.88, bf16[1,2,4096,1024]{3,2,1,0:T(8,128)(2,1)} %param.7), kind=kOutput, calls=%fused_computation.6 | convolution fusion | flops 17179869184 | bytes 33554432 | tf_op jit(solution)/shard_map/mck,dkr->mcdr/dot_general | solution.py:25
  284.0 7.3 all-to-all-start.1
  291.4 90.4 %all-to-all-done.1 = f32[8,64,2,1024]{3,1,2,0:T(8,128)} async-done(((f32[8,64,2,1024]{3,1,2,0:T(8,128)}), f32[8,64,2,1024]{3,1,2,0:T(8,128)}, u32[]{:S(2)}, u32[]{:S(2)}) %all-to-all-start.1) | async-done | bytes 4194336 | tf_op jit(solution)/shard_map/all_to_all | solution.py:65
  381.8 7.4 copy.234
  389.1 5.1 gather_fusion.1
  407.8 129.0 %while.1 = (s32[]{:T(128)}, f32[64,2,1070]{2,1,0:T(2,128)S(1)}, s32[64,3]{0,1:T(4,128)S(1)}, f32[64,2,1054]{2,1,0:T(2,128)S(1)}, s32[]{:T(128)}) while((s32[]{:T(128)}, f32[64,2,1070]{2,1,0:T(2,128)S(1)}, s32[64,3]{0,1:T(4,128)S(1)}, f32[64,2,1054]{2,1,0:T(2,128)S(1)}, s32[]{:T(128)}) %tuple.55), condition=%wide.while_cond, body=%wide.while_body.sunk | while | flops 2 | bytes 18549 | solution.py:73
  536.8 12.4 fusion.16
  549.2 7.9 fusion.17
  694.3 47.1 %stack.133 = f32[64,2,31,4,256]{4,2,1,3,0:T(8,128)} concatenate(f32[64,2,1,4,256]{4,2,1,3,0:T(1,128)} %copy.266, f32[64,2,1,4,256]{4,2,1,3,0:T(1,128)} %copy.267, f32[64,2,1,4,256]{4,2,1,3,0:T(1,128)} %copy.268, f32[64,2,1,4,256]{4,2,1,3,0:T(1,128)} %copy.269, f32[64,2,1,4,256]{4,2,1,3,0:T(1,128)} %copy.270, f32[64,2,1,4,256]{4,2,1,3,0:T(1,128)} %copy.271, ...), dimensions={2} | concatenate | bytes 32505856 | tf_op jit(solution)/shard_map/stack | solution.py:78
  741.5 21.3 %convolution_bitcast_fusion = f32[64,4,31,31]{3,2,1,0:T(8,128)} fusion(f32[64,2,31,4,256]{4,2,1,3,0:T(8,128)} %stack.133), kind=kOutput, calls=%fused_computation.13 | convolution fusion | flops 1511522304 | bytes 17236992 | tf_op jit(solution)/shard_map/scjwt,sckwt->swjk/dot_general | solution.py:80
  762.7 6.0 copy.297
  768.8 6.9 fusion.3
  775.7 728.1 %custom-call.11 = f32[64,4,31,31]{3,2,1,0:T(8,128)} custom-call(f32[64,4,31,31]{3,2,1,0:T(8,128)} %fusion.3), custom_call_target="Cholesky" | custom-call | tf_op jit(solution)/shard_map/jit(cholesky)/cholesky | solution.py:83
  1509.6 47.6 %custom-call.12 = f32[64,4,1,31,31]{0,3,4,2,1:T(8,128)S(1)} custom-call(f32[64,4,1,31,31]{0,4,3,2,1:T(8,128)} %select_bitcast_fusion), custom_call_target="InvertDiagBlocksLowerTriangular" | custom-call | tf_op jit(solution)/shard_map/jit(_cho_solve)/vmap(vmap())/triangular_solve | solution.py:84
  1557.2 4.6 copy.307
  1561.9 11.8 convolution_bitcast_fusion.3
  1577.3 6.6 convolution_bitcast_fusion.1
  1583.9 12.7 fusion.19
  (312 shorter events, 300.8 us)
Async XLA Ops:
  284.0 7.3 copy-start.5
  284.0 97.7 %all-to-all-start.1 = ((f32[8,64,2,1024]{3,1,2,0:T(8,128)}), f32[8,64,2,1024]{3,1,2,0:T(8,128)}, u32[]{:S(2)}, u32[]{:S(2)}) async-start(f32[8,64,2,1024]{3,1,2,0:T(8,128)} %pad_maximum_fusion), calls=%async_computation.1 | async-start | bytes 8388608 | tf_op jit(solution)/shard_map/all_to_all | solution.py:65
  389.1 12.5 copy-start.4
  395.2 154.0 %copy-start.1 = (f32[64,2,1024]{2,1,0:T(2,128)}, f32[64,2,1024]{2,1,0:T(2,128)S(1)}, u32[]{:S(2)}) copy-start(f32[64,2,1024]{2,1,0:T(2,128)S(1)} %bitcast_reduce_fusion) | copy-start | bytes 1572868
  395.3 7.4 collective-permute-start
  398.7 7.1 collective-permute-start.1
  557.1 12.0 copy-start.2
  1561.9 11.8 copy-start
  1583.9 12.7 copy-start.3
where the time goes:
time: 1620 us; the launch traced here: 1600 us
  other arithmetic  798 us (49%)
  local copies, waits for them, and re-layouts  426 us (26%)
  blocking collectives  188 us (12%)
  waiting for transfers between devices  93.4 us (6%)
  matrix products  77.4 us (5%)
    another operation x4, other arithmetic, body(): factor = jnp.linalg.cholesky(gram)  728 us
    all_to_all x1, blocking collectives, body(): lax.all_to_all(outgoing, 'shot', split_axis=0, concat_axis=0, tiled=True)  188 us
    another operation x63, local copies, waits for them, and re-layouts, body(): jnp.stack([aligned[:, :, tap:tap + recv_width] for tap in range(TAPS)], a...  184 us
    gather x192, local copies, waits for them, and re-layouts  129 us
    all_to_all x1, waiting for transfers between devices, body(): lax.all_to_all(products, 'shot', split_axis=0, concat_axis=0, tiled=True)  90.4 us
    another operation x3, other arithmetic, body(): jax.scipy.linalg.cho_solve((factor, True), moment[..., None])[..., 0]  49.4 us
    gather x2, local copies, waits for them, and re-layouts, body(): rows_flat[source] * filled[:, None, None]  40.8 us
  transfers between devices with their start and end apart: 3, of which 2 were waited for; matrix products, arithmetic and copies ran while one was open for 0% of the time, Pallas kernels for 0%

commit v1 on v0

v1 whole, which is shorter than its diff:
```python
import jax
import jax.numpy as jnp
from jax import lax
from jax.experimental import pallas as pl
from jax.experimental.pallas import tpu as pltpu
from jax.sharding import PartitionSpec as P

TAPS = 31
WL = 256
LAG = 8
EDGE = (TAPS - 1) // 2 + LAG
LANES = 128
HALF = WL // 2


def fit_kernel(low_ref, main_ref, high_ref, rec_ref, shift_ref, out_ref, piece, ext, raw, tgt, gram, res):
    comps, shots, width = main_ref.shape
    windows = width // WL
    span = 3 * LANES
    rows = comps * windows
    half_lanes = LANES // 2

    def block_of(c, b):
        if b == 0:
            return low_ref[c]
        if b == width // LANES + 1:
            return high_ref[c]
        return main_ref[c, :, (b - 1) * LANES : b * LANES]

    for c in range(comps):
        blocks = [block_of(c, b) for b in range(width // LANES + 2)]
        turned = [
            jnp.concatenate([blocks[b], blocks[b + 1]], axis=0).T for b in range(width // LANES + 1)
        ]
        for w in range(windows):
            g = c * windows + w
            for b in range(3):
                base = g * span + b * LANES
                piece[base : base + LANES, :] = turned[2 * w + b]
            pair = jnp.concatenate(
                [
                    rec_ref[c, :, w * WL : w * WL + HALF],
                    rec_ref[c, :, w * WL + HALF : (w + 1) * WL],
                ],
                axis=0,
            ).astype(jnp.float32)
            tgt[g * HALF : (g + 1) * HALF, :] = pair.T

    first = LANES - EDGE
    need = HALF + TAPS - 1
    top = need + 2 * LAG
    lag_of = jnp.broadcast_to(shift_ref[...], (rows, LANES))

    for i in range(top):
        raw[i] = piece[pl.ds(first + i, rows, stride=span), :]
    bit = [(lag_of & (1 << n)) != 0 for n in range(5)]
    count = need + 14
    for i in range(count):
        ext[i] = jnp.where(bit[0], raw[i + 1], raw[i])
    for n in range(1, 4):
        count -= 1 << n
        for i in range(count):
            ext[i] = jnp.where(bit[n], ext[i + (1 << n)], ext[i])
    for i in range(need):
        ext[i] = jnp.where(bit[4], raw[i + 16], ext[i])

    def total(v):
        v = v + pltpu.roll(v, rows // 2, 0)
        return v + pltpu.roll(v, half_lanes, 1)

    zero = jnp.zeros((rows, LANES), jnp.float32)
    unroll = 2

    def core(step, acc):
        i = TAPS - 1 + step * unroll
        vals = [ext[i + n] for n in range(TAPS + unroll - 1)]
        for n in range(unroll):
            acc = tuple(acc[d] + vals[n] * vals[n + d] for d in range(TAPS))
        return acc

    cores = lax.fori_loop(0, (HALF - TAPS + 1) // unroll, core, (zero,) * TAPS)
    for d in range(TAPS):
        last = TAPS - 1 - d
        run = cores[d]
        heads = [None] * (last + 1)
        if last == TAPS - 1:
            heads[last] = run
        for i in range(TAPS - 2, -1, -1):
            run = run + ext[i] * ext[i + d]
            if i <= last:
                heads[i] = run
        tail = zero
        for j in range(last + 1):
            if j > 0:
                tail = tail + ext[HALF + j - 1] * ext[HALF + j - 1 + d]
            value = total(heads[j] + tail)
            gram[j, j + d] = value + 1.0 if d == 0 else value

    def moments(step, acc):
        i = step * unroll
        vals = [ext[i + n] for n in range(TAPS + unroll - 1)]
        for n in range(unroll):
            row = tgt[pl.ds(i + n, rows, stride=HALF), :]
            acc = tuple(acc[j] + row * vals[n + j] for j in range(TAPS))
        return acc

    sums = lax.fori_loop(0, HALF // unroll, moments, (zero,) * TAPS)
    for j in range(TAPS):
        gram[j, TAPS] = total(sums[j])

    inverse = []
    for col in range(TAPS):
        rows_here = tuple(gram[col, r] for r in range(col, TAPS + 1))
        if col:

            def reduce(k, acc, col=col):
                mult = gram[k, col] * res[k]
                return tuple(acc[r - col] - mult * gram[k, r] for r in range(col, TAPS + 1))

            rows_here = lax.fori_loop(0, col, reduce, rows_here)
        for r in range(col, TAPS + 1):
            gram[col, r] = rows_here[r - col]
        res[col] = 1.0 / rows_here[0]

    left = [gram[k, TAPS] for k in range(TAPS)]
    taps = [None] * TAPS
    for r in range(TAPS - 1, -1, -1):
        taps[r] = left[r] * res[r]
        for k in range(r):
            left[k] = left[k] - gram[k, r] * taps[r]

    def subtract(step, carry):
        i = step * unroll
        vals = [ext[i + n] for n in range(TAPS + unroll - 1)]
        for n in range(unroll):
            value = tgt[pl.ds(i + n, rows, stride=HALF), :]
            fit = [zero, zero, zero, zero]
            for j in range(TAPS):
                fit[j % 4] = fit[j % 4] + carry[j] * vals[n + j]
            value = value - ((fit[0] + fit[1]) + (fit[2] + fit[3]))
            tgt[pl.ds(i + n, rows, stride=HALF), :] = value
        return carry

    lax.fori_loop(0, HALF // unroll, subtract, tuple(taps))
    for c in range(comps):
        for w in range(windows):
            g = c * windows + w
            both = tgt[g * HALF : (g + 1) * HALF, :].T
            out_ref[c, :, w * WL : w * WL + HALF] = both[:half_lanes]
            out_ref[c, :, w * WL + HALF : (w + 1) * WL] = both[half_lanes:]


def fit(low, main, high, rec, shift):
    comps, shots, width = main.shape
    rows = comps * (width // WL)
    span = 3 * LANES
    top = HALF + TAPS - 1 + 2 * LAG
    lanes_shift = jnp.tile(shift, LANES // shots)[None, :]
    vec = lambda n: pltpu.VMEM((n, rows, LANES), jnp.float32)
    return pl.pallas_call(
        fit_kernel,
        out_shape=jax.ShapeDtypeStruct(main.shape, jnp.float32),
        in_specs=[pl.BlockSpec(memory_space=pltpu.VMEM)] * 5,
        out_specs=pl.BlockSpec(memory_space=pltpu.VMEM),
        scratch_shapes=[
            pltpu.VMEM((rows * span, LANES), jnp.float32),
            vec(top),
            vec(top),
            pltpu.VMEM((rows * HALF, LANES), jnp.float32),
            pltpu.VMEM((TAPS, TAPS + 1, rows, LANES), jnp.float32),
            vec(TAPS),
        ],
        compiler_params=pltpu.CompilerParams(vmem_limit_bytes=32 * 1024 * 1024),
    )(low, main, high, rec, lanes_shift)


def product_kernel(order_ref, *refs):
    pieces = refs[:-4]
    panel_ref, out_ref, by_real, by_imag = refs[-4:]
    groups, comps, shots, width = out_ref.shape
    step = pl.program_id(1)
    real, imag = panel_ref[0], panel_ref[1]

    @pl.when(step == 0)
    def _():
        by_real[...] = jnp.zeros_like(by_real)
        by_imag[...] = jnp.zeros_like(by_imag)

    for n, piece in enumerate(pieces):

        @pl.when(step == n)
        def _(piece=piece):
            rows = piece[...].reshape(groups * comps * shots, piece.shape[-1])
            by_real[...] += jnp.dot(rows, real, preferred_element_type=jnp.float32)
            by_imag[...] += jnp.dot(rows, imag, preferred_element_type=jnp.float32)

    @pl.when(step == pl.num_programs(1) - 1)
    def _():
        for g in range(groups):
            at = 2 * g * shots
            out_ref[g, 0] = by_real[at : at + shots] - by_imag[at + shots : at + 2 * shots]
            out_ref[g, 1] = by_imag[at : at + shots] + by_real[at + shots : at + 2 * shots]


def products(pieces, order, panel):
    groups, comps, shots, depth = pieces[0].shape
    width = panel.shape[3]
    tile = width // 2
    rows = groups * comps * shots
    grid_spec = pltpu.PrefetchScalarGridSpec(
        num_scalar_prefetch=1,
        grid=(width // tile, len(pieces)),
        in_specs=[pl.BlockSpec(pieces[0].shape, lambda n, k, o: (0, 0, 0, 0))] * len(pieces)
        + [pl.BlockSpec((None, 2, depth, tile), lambda n, k, o: (0, 0, o[k], n))],
        out_specs=pl.BlockSpec((groups, comps, shots, tile), lambda n, k, o: (0, 0, 0, n)),
        scratch_shapes=[pltpu.VMEM((rows, tile), jnp.float32)] * 2,
    )
    return pl.pallas_call(
        product_kernel,
        grid_spec=grid_spec,
        out_shape=jax.ShapeDtypeStruct((groups, comps, shots, width), jnp.float32),
        compiler_params=pltpu.CompilerParams(vmem_limit_bytes=48 * 1024 * 1024),
        cost_estimate=pl.CostEstimate(
            flops=4 * rows * depth * len(pieces) * width,
            bytes_accessed=4 * depth * len(pieces) * width,
            transcendentals=0,
        ),
    )(order, *pieces, panel)


def predict_dense(shot_rows, aperture, panel):
    panel_count = lax.axis_size("shot")
    parts = lax.axis_size("sec") * lax.axis_size("win")
    depth = shot_rows.shape[3] // parts
    part = lax.axis_index("sec") * lax.axis_size("win") + lax.axis_index("win")
    mine = lax.dynamic_slice_in_dim(shot_rows, part * depth, depth, 3)
    mine = mine.transpose(1, 2, 0, 3)
    named = aperture.T[None] == jnp.arange(panel_count, dtype=jnp.int32)[:, None, None]
    outgoing = jnp.zeros((panel_count,) + mine.shape[1:], mine.dtype)
    for a in range(mine.shape[0]):
        outgoing = jnp.where(named[:, a, None, :, None], mine[a][None], outgoing)
    own = lax.all_to_all(outgoing, "shot", split_axis=0, concat_axis=0, tiled=True)
    swap = [(0, 1), (1, 0)]
    half = panel_count // 2
    by_sec = lax.ppermute(own, "sec", swap)
    by_win = lax.ppermute(own, "win", swap)
    both = jnp.concatenate(
        [lax.ppermute(by_sec[:half], "win", swap), lax.ppermute(by_win[half:], "sec", swap)], axis=0
    )
    order = jnp.bitwise_xor(part, jnp.array([0, 1, 2, 3], jnp.int32)).astype(jnp.int32)
    terms = products((own, by_win, by_sec, both), order, panel)
    return lax.psum_scatter(terms, "shot", scatter_dimension=0, tiled=True)[0]


def predict_slots(shot_rows, aperture, panel, capacity):
    shot_count, slot_count = aperture.shape
    row_count = shot_count * slot_count
    trace_width = shot_rows.shape[3]
    recv_width = panel.shape[3]
    panel_count = lax.axis_size("shot")
    weights = panel[0]
    ap_flat = aperture.reshape(row_count)
    indicator = (ap_flat[:, None] == jnp.arange(panel_count, dtype=jnp.int32)[None, :]).astype(
        jnp.int32
    )
    earlier = jnp.cumsum(indicator, axis=0) - indicator
    position = jnp.sum(earlier * indicator, axis=1)
    slot_id = ap_flat * capacity + position
    source = (
        jnp.zeros((panel_count * capacity,), jnp.int32)
        .at[slot_id]
        .set(jnp.arange(row_count, dtype=jnp.int32))
    )
    rows_flat = shot_rows.reshape(row_count, 2, trace_width)
    outgoing = rows_flat[source].reshape(panel_count, capacity, 2, trace_width)
    received = lax.all_to_all(outgoing, "shot", split_axis=0, concat_axis=0, tiled=True)
    stacked = received.reshape(panel_count * capacity, 2, trace_width)
    parts = jnp.einsum("mck,dkr->mcdr", stacked, weights, preferred_element_type=jnp.float32)
    real_part = parts[:, 0, 0] - parts[:, 1, 1]
    imag_part = parts[:, 0, 1] + parts[:, 1, 0]
    terms = jnp.stack([real_part, imag_part], axis=1)
    terms = terms.reshape(panel_count, capacity, 2, recv_width)
    returned = lax.all_to_all(terms, "shot", split_axis=0, concat_axis=0, tiled=True)
    back_flat = returned.reshape(panel_count * capacity, 2, recv_width)
    predicted = jnp.sum(back_flat[slot_id].reshape(shot_count, slot_count, 2, recv_width), axis=1)
    return predicted.transpose(1, 0, 2)


def body(shot_rows, aperture, panel, recorded, shift):
    shot_count, slot_count = aperture.shape
    capacity = 2 * shot_count * slot_count // lax.axis_size("shot")
    if capacity >= shot_count:
        predicted = predict_dense(shot_rows, aperture, panel)
    else:
        predicted = predict_slots(shot_rows, aperture, panel, capacity)
    count = lax.axis_size(("sec", "win"))
    forward = [(i, i + 1) for i in range(count - 1)]
    backward = [(target, source) for source, target in forward]
    low = lax.ppermute(predicted[:, :, -LANES:], ("sec", "win"), forward)
    high = lax.ppermute(predicted[:, :, :LANES], ("sec", "win"), backward)
    primaries = fit(low, predicted, high, recorded.transpose(1, 0, 2), shift)
    return (predicted.transpose(1, 0, 2), primaries.transpose(1, 0, 2))


def solution(mesh):
    in_specs = (
        P("shot", None, None, None),
        P("shot", None),
        P("shot", None, None, ("sec", "win")),
        P("shot", None, ("sec", "win")),
        P("shot"),
    )
    out_specs = (P("shot", None, ("sec", "win")), P("shot", None, ("sec", "win")))
    return jax.shard_map(body, mesh=mesh, in_specs=in_specs, out_specs=out_specs, check_vma=False)
```

time: 1620 us -> 246 us (0.15); the launches traced: 1600 us -> 242 us
  other arithmetic: 798 us -> 2.31 us
  local copies, waits for them, and re-layouts: 426 us -> 7.77 us
  blocking collectives: 188 us -> 51.8 us
  matrix products: 77.4 us -> 0 us
  Pallas kernels: 0 us -> 37.3 us
  waiting for transfers between devices: 93.4 us -> 119 us
    another operation x10 -> x0, other arithmetic: 781 us -> none  [the longest x4 728 us: body(): factor = jnp.linalg.cholesky(gram)]
    another operation x67 -> x2, local copies, waits for them, and re-layouts: 193 us -> 0.08 us  [fit(): lanes_shift = jnp.tile(shift, LANES // shots)[None, :]]
    gather x195 -> x0, local copies, waits for them, and re-layouts: 175 us -> none
    all_to_all x1, blocking collectives: 188 us -> 51.8 us  [predict_dense(): lax.all_to_all(outgoing, 'shot', split_axis=0, concat_axis=0, tiled=True)]
    all_to_all x1 -> x0, waiting for transfers between devices: 90.4 us -> none  [body(): lax.all_to_all(products, 'shot', split_axis=0, concat_axis=0, tiled=True)]
    dot_general x4 -> x0, matrix products: 67.2 us -> none  [the longest x1 21.5 us: complex_rows(): jnp.einsum('mck,dkr->mcdr', rows_here, weights, preferred_element_type=jn...]
    ppermute x2 -> x6, waiting for transfers between devices: 2.99 us -> 69.9 us  [the longest x1 44.9 us: predict_dense(): by_sec = lax.ppermute(own, 'sec', swap)]
    reduce_scatter x0 -> x1, waiting for transfers between devices: none -> 48.9 us  [predict_dense(): return lax.psum_scatter(terms, 'shot', scatter_dimension=0, tiled=True)[0]]
  transfers between devices with their start and end apart: 3 -> 7, of which waited for: 2 -> 6; matrix products, arithmetic and copies ran while one was open for 0% -> 1% of each run, Pallas kernels for 0% -> 0%
where the time goes in v1:
time: 246 us; the launch traced here: 242 us
  waiting for transfers between devices  119 us (48%)
  blocking collectives  51.8 us (21%)
  Pallas kernels  37.3 us (15%)
  between operations  14.2 us (6%)
  starting transfers between devices  10.1 us (4%)
  local copies, waits for them, and re-layouts  7.77 us (3%)
    all_to_all x1, blocking collectives, predict_dense(): lax.all_to_all(outgoing, 'shot', split_axis=0, concat_axis=0, tiled=True)  51.8 us
    reduce_scatter x1, waiting for transfers between devices, predict_dense(): return lax.psum_scatter(terms, 'shot', scatter_dimension=0, tiled=True)[0]  48.9 us
    ppermute x1, waiting for transfers between devices, predict_dense(): by_sec = lax.ppermute(own, 'sec', swap)  44.9 us
    pallas_call x1, Pallas kernels, products(): pl.pallas_call(product_kernel, grid_spec=grid_spec, out_shape=jax.ShapeDt...  24.9 us
    ppermute x1, waiting for transfers between devices, predict_dense(): lax.ppermute(by_sec[:half], 'win', swap)  20.9 us
    pallas_call x1, Pallas kernels, fit(): pl.pallas_call(fit_kernel, out_shape=jax.ShapeDtypeStruct(main.shape, jnp...  12.4 us
  transfers between devices with their start and end apart: 7, of which 6 were waited for; matrix products, arithmetic and copies ran while one was open for 1% of the time, Pallas kernels for 0%

profile of v1, /device:TPU:12, one launch (start us, length us, event | category | flops | bytes accessed | tf_op | source)
XLA Modules:
  0.0 242.4 jit_solution(12692977269970069842)
XLA Ops:
  7.2 2.1 dynamic-slice_bitcast_fusion
  9.4 0.7 slice_bitcast_fusion.3
  10.4 0.8 select_select_fusion
  11.1 51.8 %all_to_all.5.refs_0_ = bf16[8,2,64,1024]{3,2,1,0:T(8,128)(2,1)S(1)} all-to-all(bf16[8,2,64,1024]{3,2,1,0:T(8,128)(2,1)S(1)} %select_select_fusion), channel_id=1, replica_groups=mesh['sec'=2,'shot'=8,'win'=2] {'shot'}, dimensions={0} | all-to-all | bytes 4194304 | tf_op jit(solution)/shard_map/all_to_all | solution.py:242
  62.9 1.5 collective-permute-start.1
  64.4 0.5 collective-permute-start
  64.9 44.9 %collective-permute-done.1.refs_2_ = bf16[8,2,64,1024]{3,2,1,0:T(8,128)(2,1)S(1)} collective-permute-done((bf16[8,2,64,1024]{3,2,1,0:T(8,128)(2,1)S(1)}, bf16[8,2,64,1024]{3,2,1,0:T(8,128)(2,1)S(1)}, u32[]{:S(2)}, u32[]{:S(2)}) %collective-permute-start.1) | collective-permute-done | bytes 2097184 | tf_op jit(solution)/shard_map/ppermute | solution.py:245
  110.0 0.6 collective-permute-start.2
  110.5 0.6 collective-permute-done.refs_1_
  111.1 0.1 slice.57
  111.2 1.5 collective-permute-start.3
  112.7 20.9 %collective-permute-done.2 = bf16[4,2,64,1024]{3,2,1,0:T(8,128)(2,1)S(1)} collective-permute-done((bf16[4,2,64,1024]{3,2,1,0:T(8,128)(2,1)S(1)}, bf16[4,2,64,1024]{3,2,1,0:T(8,128)(2,1)S(1)}, u32[]{:S(2)}, u32[]{:S(2)}) %collective-permute-start.2) | collective-permute-done | bytes 1048608 | tf_op jit(solution)/shard_map/ppermute | solution.py:248
  133.6 1.2 collective-permute-done.3
  134.8 1.5 pad_maximum_fusion.refs_3_
  136.3 24.9 %shard_map.77 = f32[8,2,64,1024]{3,2,1,0:T(8,128)} custom-call(s32[4]{0:T(128)S(1)} %iota_xor_fusion.order_ref, bf16[8,2,64,1024]{3,2,1,0:T(8,128)(2,1)S(1)} %all_to_all.5.refs_0_, bf16[8,2,64,1024]{3,2,1,0:T(8,128)(2,1)S(1)} %collective-permute-done.refs_1_, bf16[8,2,64,1024]{3,2,1,0:T(8,128)(2,1)} %copy-done.1, ...), custom_call_target="tpu_custom_call" | custom-call | flops 17179869184 | bytes 16777216 | tf_op jit(solution)/shard_map/pallas_call | solution.py:218
  161.2 48.9 %reduce-scatter.2.cloned.1.call-done = f32[1,2,64,1024]{3,2,1,0:T(8,128)} async-done(((f32[8,2,64,1024]{3,2,1,0:T(8,128)}), f32[1,2,64,1024]{3,2,1,0:T(8,128)}) %reduce-scatter.2.cloned.1.call-update) | async-done | bytes 524304 | tf_op jit(solution)/shard_map/reduce_scatter | solution.py:252
  210.2 0.9 fusion
  211.1 3.3 %collective-permute-start.4 = (f32[2,64,128]{2,1,0:T(8,128)S(1)}, f32[2,64,128]{2,1,0:T(8,128)S(1)}, u32[]{:S(2)}, u32[]{:S(2)}) collective-permute-start(f32[2,64,128]{2,1,0:T(8,128)S(1)} %get-tuple-element.9), channel_id=1, source_target_pairs={{0,1},{1,16},{16,17},{2,3},{3,18},{18,19},{4,5},{5,20},{20,21},{6,... | collective-permute-start | bytes 196616 | tf_op jit(solution)/shard_map/ppermute | solution.py:299
  214.5 2.7 %collective-permute-start.5 = (f32[2,64,128]{2,1,0:T(8,128)S(1)}, f32[2,64,128]{2,1,0:T(8,128)S(1)}, u32[]{:S(2)}, u32[]{:S(2)}) collective-permute-start(f32[2,64,128]{2,1,0:T(8,128)S(1)} %get-tuple-element.8), channel_id=1, source_target_pairs={{1,0},{16,1},{17,16},{3,2},{18,3},{19,18},{5,4},{20,5},{21,20},{7,... | collective-permute-start | bytes 196616 | tf_op jit(solution)/shard_map/ppermute | solution.py:300
  217.3 0.1 broadcast_in_dim_tile.3.shift_ref
  217.3 2.2 copy.13
  219.6 2.3 collective-permute-done.5.high_ref
  221.9 12.4 %shard_map.78 = f32[2,64,1024]{2,1,0:T(8,128)S(1)} custom-call(f32[2,64,128]{2,1,0:T(8,128)S(1)} %collective-permute-done.4.low_ref, f32[2,64,1024]{2,1,0:T(8,128)S(1)} %bitcast.28, f32[2,64,128]{2,1,0:T(8,128)S(1)} %collective-permute-done.5.high_ref, bf16[2,64,1024]{2,1,0:T(8,128)(2,1)S(1)} %bitcast.30, s32[1,128]{1,0:T(1,128)S(1)} %broadcast_in_dim_tile.3.shift_ref), custom_call_target="tpu_custom_call" | custom-call | tf_op jit(solution)/shard_map/pallas_call | solution.py:160
  234.4 1.2 copy.14
  (23 shorter events, 0.4 us)
Async XLA Ops:
  7.2 203.0 %reduce-scatter.2.cloned.1.call-start = ((), (), s32[]{:S(2)}) async-start(), calls=%async_computation.2 | async-start | bytes 4718592 | tf_op jit(solution)/shard_map/reduce_scatter | solution.py:252
  9.4 1.0 copy-start.3
  62.9 46.9 %collective-permute-start.1 = (bf16[8,2,64,1024]{3,2,1,0:T(8,128)(2,1)S(1)}, bf16[8,2,64,1024]{3,2,1,0:T(8,128)(2,1)S(1)}, u32[]{:S(2)}, u32[]{:S(2)}) collective-permute-start(bf16[8,2,64,1024]{3,2,1,0:T(8,128)(2,1)S(1)} %all_to_all.5.refs_0_), channel_id=1, source_target_pairs={{0,16},{16,0},{1,17},{17,1},{2,18},{18,2},{3,19},{19,3},{4,20},{20... | collective-permute-start | bytes 6291464 | tf_op jit(solution)/shard_map/ppermute | solution.py:245
  64.4 46.7 %collective-permute-start = (bf16[8,2,64,1024]{3,2,1,0:T(8,128)(2,1)S(1)}, bf16[8,2,64,1024]{3,2,1,0:T(8,128)(2,1)S(1)}, u32[]{:S(2)}, u32[]{:S(2)}) collective-permute-start(bf16[8,2,64,1024]{3,2,1,0:T(8,128)(2,1)S(1)} %all_to_all.5.refs_0_), channel_id=1, source_target_pairs={{0,1},{1,0},{2,3},{3,2},{4,5},{5,4},{6,7},{7,6},{8,9},{9,8},{10,11... | collective-permute-start | bytes 6291464 | tf_op jit(solution)/shard_map/ppermute | solution.py:246
  109.9 1.3 copy-start.1
  110.0 23.6 %collective-permute-start.2 = (bf16[4,2,64,1024]{3,2,1,0:T(8,128)(2,1)S(1)}, bf16[4,2,64,1024]{3,2,1,0:T(8,128)(2,1)S(1)}, u32[]{:S(2)}, u32[]{:S(2)}) collective-permute-start(bf16[4,2,64,1024]{3,2,1,0:T(8,128)(2,1)S(1)} %slice.56), channel_id=1, source_target_pairs={{0,1},{1,0},{2,3},{3,2},{4,5},{5,4},{6,7},{7,6},{8,9},{9,8},{10,11... | collective-permute-start | bytes 3145736 | tf_op jit(solution)/shard_map/ppermute | solution.py:248
  111.2 23.6 %collective-permute-start.3 = (bf16[4,2,64,1024]{3,2,1,0:T(8,128)(2,1)S(1)}, bf16[4,2,64,1024]{3,2,1,0:T(8,128)(2,1)S(1)}, u32[]{:S(2)}, u32[]{:S(2)}) collective-permute-start(bf16[4,2,64,1024]{3,2,1,0:T(8,128)(2,1)S(1)} %slice.57), channel_id=1, source_target_pairs={{0,16},{16,0},{1,17},{17,1},{2,18},{18,2},{3,19},{19,3},{4,20},{20... | collective-permute-start | bytes 3145736 | tf_op jit(solution)/shard_map/ppermute | solution.py:248
  161.2 55.9 %copy-start.2 = (bf16[64,2,1024]{2,1,0:T(2,128)(2,1)S(1)}, bf16[64,2,1024]{2,1,0:T(2,128)(2,1)}, u32[]{:S(2)}) copy-start(bf16[64,2,1024]{2,1,0:T(2,128)(2,1)} %param.9) | copy-start | bytes 786436
  161.2 56.0 %copy-start.4 = (s32[64]{0:T(128)S(1)}, s32[64]{0:T(128)}, u32[]{:S(2)}) copy-start(s32[64]{0:T(128)} %param.10) | copy-start | bytes 772
  210.2 11.7 %copy-start = (f32[1,2,64,1024]{3,2,1,0:T(8,128)S(1)}, f32[1,2,64,1024]{3,2,1,0:T(8,128)}, u32[]{:S(2)}) copy-start(f32[1,2,64,1024]{3,2,1,0:T(8,128)} %reduce-scatter.2.cloned.1.call-done) | copy-start | bytes 1572868
  211.1 8.4 %collective-permute-start.4 = (f32[2,64,128]{2,1,0:T(8,128)S(1)}, f32[2,64,128]{2,1,0:T(8,128)S(1)}, u32[]{:S(2)}, u32[]{:S(2)}) collective-permute-start(f32[2,64,128]{2,1,0:T(8,128)S(1)} %get-tuple-element.9), channel_id=1, source_target_pairs={{0,1},{1,16},{16,17},{2,3},{3,18},{18,19},{4,5},{5,20},{20,21},{6,... | collective-permute-start | bytes 196616 | tf_op jit(solution)/shard_map/ppermute | solution.py:299
  214.5 7.4 %collective-permute-start.5 = (f32[2,64,128]{2,1,0:T(8,128)S(1)}, f32[2,64,128]{2,1,0:T(8,128)S(1)}, u32[]{:S(2)}, u32[]{:S(2)}) collective-permute-start(f32[2,64,128]{2,1,0:T(8,128)S(1)} %get-tuple-element.8), channel_id=1, source_target_pairs={{1,0},{16,1},{17,16},{3,2},{18,3},{19,18},{5,4},{20,5},{21,20},{7,... | collective-permute-start | bytes 196616 | tf_op jit(solution)/shard_map/ppermute | solution.py:300
Sparse Core Ops, SparseCore 0:
  161.4 48.7 reduce-scatter.1

commit v2 on v1

--- a/solution.py
+++ b/solution.py
@@ -1,3 +1,5 @@
+import functools
+
 import jax
 import jax.numpy as jnp
 from jax import lax
@@ -174,8 +176,7 @@
     )(low, main, high, rec, lanes_shift)
 
 
-def product_kernel(order_ref, *refs):
-    pieces = refs[:-4]
+def product_kernel(order_ref, *refs, layout, has_base):
     panel_ref, out_ref, by_real, by_imag = refs[-4:]
     groups, comps, shots, width = out_ref.shape
     step = pl.program_id(1)
@@ -186,70 +187,218 @@
         by_real[...] = jnp.zeros_like(by_real)
         by_imag[...] = jnp.zeros_like(by_imag)
 
-    for n, piece in enumerate(pieces):
-
-        @pl.when(step == n)
-        def _(piece=piece):
-            rows = piece[...].reshape(groups * comps * shots, piece.shape[-1])
-            by_real[...] += jnp.dot(rows, real, preferred_element_type=jnp.float32)
-            by_imag[...] += jnp.dot(rows, imag, preferred_element_type=jnp.float32)
+    def add(pieces):
+        flat = [piece[...].reshape(-1, piece.shape[-1]) for piece in pieces]
+        rows = jnp.concatenate(flat, axis=0) if len(flat) > 1 else flat[0]
+        by_real[...] += jnp.dot(rows, real, preferred_element_type=jnp.float32)
+        by_imag[...] += jnp.dot(rows, imag, preferred_element_type=jnp.float32)
+
+    at = 0
+    for n, count in enumerate(layout):
+        pieces = refs[at : at + count]
+        at += count
+        pl.when(step == n)(functools.partial(add, pieces))
 
     @pl.when(step == pl.num_programs(1) - 1)
     def _():
         for g in range(groups):
-            at = 2 * g * shots
-            out_ref[g, 0] = by_real[at : at + shots] - by_imag[at + shots : at + 2 * shots]
-            out_ref[g, 1] = by_imag[at : at + shots] + by_real[at + shots : at + 2 * shots]
-
-
-def products(pieces, order, panel):
-    groups, comps, shots, depth = pieces[0].shape
-    width = panel.shape[3]
+            row = 2 * g * shots
+            real_part = by_real[row : row + shots] - by_imag[row + shots : row + 2 * shots]
+            imag_part = by_imag[row : row + shots] + by_real[row + shots : row + 2 * shots]
+            if has_base:
+                real_part += refs[at][g, 0]
+                imag_part += refs[at][g, 1]
+            out_ref[g, 0] = real_part
+            out_ref[g, 1] = imag_part
+
+
+def products(pieces, order, panel, depth, base=None):
+    _, comps, _, width = panel.shape
+    parts = len(pieces)
     tile = width // 2
+    shots = pieces[0][0].shape[2]
+    groups = sum(piece.shape[0] for piece in pieces[0])
     rows = groups * comps * shots
+    flat = [piece for part in pieces for piece in part]
+    specs = []
+    for at, part in enumerate(pieces):
+        for piece in part:
+            block = at if piece.shape[3] > depth else 0
+            specs.append(
+                pl.BlockSpec(piece.shape[:3] + (depth,), lambda n, k, o, block=block: (0, 0, 0, block))
+            )
+    out_spec = pl.BlockSpec((groups, comps, shots, tile), lambda n, k, o: (0, 0, 0, n))
+    if base is not None:
+        flat.append(base)
+        specs.append(out_spec)
     grid_spec = pltpu.PrefetchScalarGridSpec(
         num_scalar_prefetch=1,
-        grid=(width // tile, len(pieces)),
-        in_specs=[pl.BlockSpec(pieces[0].shape, lambda n, k, o: (0, 0, 0, 0))] * len(pieces)
-        + [pl.BlockSpec((None, 2, depth, tile), lambda n, k, o: (0, 0, o[k], n))],
-        out_specs=pl.BlockSpec((groups, comps, shots, tile), lambda n, k, o: (0, 0, 0, n)),
+        grid=(width // tile, parts),
+        in_specs=specs
+        + [pl.BlockSpec((None, comps, depth, tile), lambda n, k, o: (0, 0, o[k], n))],
+        out_specs=out_spec,
         scratch_shapes=[pltpu.VMEM((rows, tile), jnp.float32)] * 2,
     )
     return pl.pallas_call(
-        product_kernel,
+        functools.partial(
+            product_kernel,
+            layout=tuple(len(part) for part in pieces),
+            has_base=base is not None,
+        ),
         grid_spec=grid_spec,
         out_shape=jax.ShapeDtypeStruct((groups, comps, shots, width), jnp.float32),
-        compiler_params=pltpu.CompilerParams(vmem_limit_bytes=48 * 1024 * 1024),
+        compiler_params=pltpu.CompilerParams(vmem_limit_bytes=52 * 1024 * 1024),
         cost_estimate=pl.CostEstimate(
-            flops=4 * rows * depth * len(pieces) * width,
-            bytes_accessed=4 * depth * len(pieces) * width,
+            flops=4 * rows * depth * parts * width,
+            bytes_accessed=4 * depth * parts * width,
             transcendentals=0,
         ),
-    )(order, *pieces, panel)
+    )(order, *flat, panel)
+
+
+CODES = 32766.0
+FINE = 256.0
+
+
+def code_kernel(first_ref, second_ref, out_ref):
+    comps, shots, width = first_ref.shape
+    blocks = width // LANES
+    for c in range(comps):
+        rows = slice(c * shots, (c + 1) * shots)
+        lane = lax.broadcasted_iota(jnp.int32, (shots, LANES), 1)
+        peak = jnp.full((shots, LANES), 2.0**-100, jnp.float32)
+        sums = []
+        for b in range(blocks):
+            at = slice(b * LANES, (b + 1) * LANES)
+            value = first_ref[c, :, at] + second_ref[c, :, at]
+            sums.append(value)
+            most = jnp.max(jnp.abs(value), axis=1, keepdims=True)
+            peak = jnp.where(lane == b, jnp.maximum(peak, most), peak)
+        power = jnp.ceil(jnp.log2(peak) * FINE)
+        scale = jnp.exp2(power * (-1.0 / FINE)) * CODES
+        for b in range(blocks):
+            at = slice(b * LANES, (b + 1) * LANES)
+            code = jnp.round(sums[b] * scale[:, b : b + 1])
+            code = jnp.clip(code, -32767.0, 32767.0)
+            out_ref[rows, at] = code.astype(jnp.int32).astype(jnp.int16)
+        out_ref[rows, width:] = power.astype(jnp.int32).astype(jnp.int16)
+
+
+def coded(first, second):
+    comps, shots, width = first.shape
+    return pl.pallas_call(
+        code_kernel,
+        out_shape=jax.ShapeDtypeStruct((comps * shots, width + LANES), jnp.int16),
+        in_specs=[pl.BlockSpec(memory_space=pltpu.VMEM)] * 2,
+        out_specs=pl.BlockSpec(memory_space=pltpu.VMEM),
+        compiler_params=pltpu.CompilerParams(vmem_limit_bytes=16 * 1024 * 1024),
+    )(first, second)
+
+
+def sum_kernel(first_ref, second_ref, *refs):
+    codes = refs[:-3]
+    out_ref, start_ref, end_ref = refs[-3:]
+    comps, shots, width = first_ref.shape
+    blocks = width // LANES
+    for c in range(comps):
+        rows = slice(c * shots, (c + 1) * shots)
+        scales = []
+        for code in codes:
+            power = code[rows, width:].astype(jnp.int32).astype(jnp.float32)
+            scales.append(jnp.exp2(power * (1.0 / FINE)) * (1.0 / CODES))
+        for b in range(blocks):
+            at = slice(b * LANES, (b + 1) * LANES)
+            value = first_ref[c, :, at] + second_ref[c, :, at]
+            for code, scale in zip(codes, scales):
+                part = code[rows, at].astype(jnp.int32).astype(jnp.float32)
+                value = value + part * scale[:, b : b + 1]
+            out_ref[c, :, at] = value
+            if b == 0:
+                start_ref[c] = value
+            if b == blocks - 1:
+                end_ref[c] = value
+
+
+def summed(first, second, codes):
+    comps, shots, width = first.shape
+    end = jax.ShapeDtypeStruct((comps, shots, LANES), jnp.float32)
+    return pl.pallas_call(
+        sum_kernel,
+        out_shape=(jax.ShapeDtypeStruct(first.shape, jnp.float32), end, end),
+        in_specs=[pl.BlockSpec(memory_space=pltpu.VMEM)] * (2 + len(codes)),
+        out_specs=(pl.BlockSpec(memory_space=pltpu.VMEM),) * 3,
+        compiler_params=pltpu.CompilerParams(vmem_limit_bytes=16 * 1024 * 1024),
+    )(first, second, *codes)
+
+
+def chosen(rows, aperture, panels):
+    named = aperture.T[None] == panels[:, None, None]
+    out = jnp.zeros((panels.shape[0],) + rows.shape[1:], rows.dtype)
+    for a in range(rows.shape[0]):
+        out = jnp.where(named[:, a, None, :, None], rows[a][None], out)
+    return out
 
 
 def predict_dense(shot_rows, aperture, panel):
     panel_count = lax.axis_size("shot")
+    me = lax.axis_index("shot")
     parts = lax.axis_size("sec") * lax.axis_size("win")
     depth = shot_rows.shape[3] // parts
     part = lax.axis_index("sec") * lax.axis_size("win") + lax.axis_index("win")
-    mine = lax.dynamic_slice_in_dim(shot_rows, part * depth, depth, 3)
-    mine = mine.transpose(1, 2, 0, 3)
-    named = aperture.T[None] == jnp.arange(panel_count, dtype=jnp.int32)[:, None, None]
-    outgoing = jnp.zeros((panel_count,) + mine.shape[1:], mine.dtype)
-    for a in range(mine.shape[0]):
-        outgoing = jnp.where(named[:, a, None, :, None], mine[a][None], outgoing)
-    own = lax.all_to_all(outgoing, "shot", split_axis=0, concat_axis=0, tiled=True)
-    swap = [(0, 1), (1, 0)]
-    half = panel_count // 2
-    by_sec = lax.ppermute(own, "sec", swap)
-    by_win = lax.ppermute(own, "win", swap)
-    both = jnp.concatenate(
-        [lax.ppermute(by_sec[:half], "win", swap), lax.ppermute(by_win[half:], "sec", swap)], axis=0
-    )
-    order = jnp.bitwise_xor(part, jnp.array([0, 1, 2, 3], jnp.int32)).astype(jnp.int32)
-    terms = products((own, by_win, by_sec, both), order, panel)
-    return lax.psum_scatter(terms, "shot", scatter_dimension=0, tiled=True)[0]
+
+    def partner(value, step):
+        return lax.ppermute(value, "shot", [(i, i ^ step) for i in range(panel_count)])
+
+    def across(value, axis):
+        return lax.ppermute(value, axis, [(0, 1), (1, 0)])
+
+    fence = lax.optimization_barrier
+    order = jnp.bitwise_xor(part, jnp.arange(parts, dtype=jnp.int32))
+
+    def turned(rows, n):
+        here = lax.dynamic_slice_in_dim(rows, order[n] * depth, depth, 3)
+        return here.transpose(1, 2, 0, 3)
+
+    def panels(steps):
+        return jnp.bitwise_xor(me, jnp.array(steps, jnp.int32))
+
+    def exchange(far, steps):
+        got = [partner(far[n : n + 1], k) for n, k in enumerate(steps)]
+        return jnp.concatenate(got, axis=0)
+
+    cut = 2 * ((panel_count + 2) // 4 + 1)
+    early, late = list(range(2, cut)), list(range(cut, panel_count))
+    mine = turned(shot_rows, 0)
+    far = chosen(mine, aperture, panels(early + late))
+    own = exchange(far, early)
+    far, shot_rows, own = fence((far, shot_rows, own))
+    by_sec, by_win = across(own, "sec"), across(own, "win")
+    own_late = exchange(far[len(early) :], late)
+    pieces = [turned(shot_rows, n) for n in range(parts)]
+    local = [chosen(piece, aperture, panels([0, 1])) for piece in pieces]
+    sibling = [partner(jnp.concatenate([piece[1:] for piece in local], axis=0), 1)]
+    half = len(early) // 2
+    both = (across(by_sec[:half], "win"), across(by_win[half:], "sec"))
+    late_sec, late_win = across(own_late, "sec"), across(own_late, "win")
+    exchanged = ((own,), (by_win,), (by_sec,), both)
+    lists = [
+        (local[n][:1], sibling[0][n : n + 1]) + tuple(exchanged[n]) for n in range(parts)
+    ]
+    terms = products(lists, order, panel, depth)
+    late_sec, late_win, terms = fence((late_sec, late_win, terms))
+    half = len(late) // 2
+    late_both = (across(late_sec[:half], "win"), across(late_win[half:], "sec"))
+    most = products(((own_late,), (late_win,), (late_sec,)), order[:3], panel, depth)
+    others = [partner(terms[n + 1], 1) for n in range(0, 2 + len(early), 2)]
+    codes = [coded(terms[2 * n], others[n]) for n in range(1, 1 + len(early) // 2)]
+    late_both, codes, others = fence((late_both, codes, others))
+    last = products((late_both,), order[3:], panel, depth, most)
+    codes = [partner(code, k) for code, k in zip(codes, early[::2])]
+    late_others = [partner(last[n + 1], 1) for n in range(0, len(late), 2)]
+    late_others, codes = fence((late_others, codes))
+    for n, k in enumerate(late[::2]):
+        codes.append(partner(coded(last[2 * n], late_others[n]), k))
+    return summed(terms[0], others[0], codes)
 
 
 def predict_slots(shot_rows, aperture, panel, capacity):
@@ -289,15 +438,17 @@
 def body(shot_rows, aperture, panel, recorded, shift):
     shot_count, slot_count = aperture.shape
     capacity = 2 * shot_count * slot_count // lax.axis_size("shot")
-    if capacity >= shot_count:
-        predicted = predict_dense(shot_rows, aperture, panel)
+    columns = (lax.axis_size("sec"), lax.axis_size("win"))
+    if capacity >= shot_count and lax.axis_size("shot") > 4 and columns == (2, 2):
+        predicted, start, end = predict_dense(shot_rows, aperture, panel)
     else:
         predicted = predict_slots(shot_rows, aperture, panel, capacity)
+        start, end = predicted[:, :, :LANES], predicted[:, :, -LANES:]
     count = lax.axis_size(("sec", "win"))
     forward = [(i, i + 1) for i in range(count - 1)]
     backward = [(target, source) for source, target in forward]
-    low = lax.ppermute(predicted[:, :, -LANES:], ("sec", "win"), forward)
-    high = lax.ppermute(predicted[:, :, :LANES], ("sec", "win"), backward)
+    low = lax.ppermute(end, ("sec", "win"), forward)
+    high = lax.ppermute(start, ("sec", "win"), backward)
     primaries = fit(low, predicted, high, recorded.transpose(1, 0, 2), shift)
     return (predicted.transpose(1, 0, 2), primaries.transpose(1, 0, 2))
 

time: 246 us -> 178 us (0.72); the launches traced: 242 us -> 177 us
  blocking collectives: 51.8 us -> 0 us
  waiting for transfers between devices: 119 us -> 71.7 us
  starting transfers between devices: 10.1 us -> 26.2 us
  local copies, waits for them, and re-layouts: 7.77 us -> 21.8 us
  Pallas kernels: 37.3 us -> 49.8 us
  between operations: 14.2 us -> 3.74 us
    all_to_all x1 -> x0, blocking collectives: 51.8 us -> none  [predict_dense(): lax.all_to_all(outgoing, 'shot', split_axis=0, concat_axis=0, tiled=True)]
    reduce_scatter x1 -> x0, waiting for transfers between devices: 48.9 us -> none  [predict_dense(): return lax.psum_scatter(terms, 'shot', scatter_dimension=0, tiled=True)[0]]
    ppermute x6 -> x24, starting transfers between devices: 10.1 us -> 26.2 us  [the longest x14 10.9 us: partner(): lax.ppermute(value, 'shot', [(i, i ^ step) for i in range(panel_count)])]
    pallas_call x1 -> x7, Pallas kernels: 24.9 us -> 37.3 us  [the longest x3 35 us: products(): pl.pallas_call(functools.partial(product_kernel, layout=tuple((len(part)...]
    transpose x1 -> x2, local copies, waits for them, and re-layouts: 2.13 us -> 8.25 us  [turned(): return here.transpose(1, 2, 0, 3)]
    broadcast_in_dim x6 -> x25, local copies, waits for them, and re-layouts: 0.92 us -> 5.87 us  [chosen(): out = jnp.where(named[:, a, None, :, None], rows[a][None], out)]
    ppermute x6 -> x24, waiting for transfers between devices: 69.9 us -> 71.7 us  [the longest x14 59.5 us: partner(): lax.ppermute(value, 'shot', [(i, i ^ step) for i in range(panel_count)])]
  transfers between devices with their start and end apart: 7 -> 24, of which waited for: 6 -> 10; matrix products, arithmetic and copies ran while one was open for 1% -> 8% of each run, Pallas kernels for 0% -> 18%
where the time goes in v2:
time: 178 us; the launch traced here: 177 us
  waiting for transfers between devices  71.7 us (40%)
  Pallas kernels  49.8 us (28%)
  starting transfers between devices  26.2 us (15%)
  local copies, waits for them, and re-layouts  21.8 us (12%)
  other arithmetic  4.04 us (2%)
  between operations  3.74 us (2%)
    ppermute x14, waiting for transfers between devices, partner(): lax.ppermute(value, 'shot', [(i, i ^ step) for i in range(panel_count)])  59.5 us
    pallas_call x3, Pallas kernels, products(): pl.pallas_call(functools.partial(product_kernel, layout=tuple((len(part)...  35 us
    pallas_call x1, Pallas kernels, fit(): pl.pallas_call(fit_kernel, out_shape=jax.ShapeDtypeStruct(main.shape, jnp...  12.4 us
    ppermute x14, starting transfers between devices, partner(): lax.ppermute(value, 'shot', [(i, i ^ step) for i in range(panel_count)])  10.9 us
    ppermute x8, starting transfers between devices, across(): return lax.ppermute(value, axis, [(0, 1), (1, 0)])  9.44 us
    ppermute x8, waiting for transfers between devices, across(): return lax.ppermute(value, axis, [(0, 1), (1, 0)])  8.98 us
    transpose x2, local copies, waits for them, and re-layouts, turned(): return here.transpose(1, 2, 0, 3)  8.25 us
    broadcast_in_dim x25, local copies, waits for them, and re-layouts, chosen(): out = jnp.where(named[:, a, None, :, None], rows[a][None], out)  5.87 us
  transfers between devices with their start and end apart: 24, of which 10 were waited for; matrix products, arithmetic and copies ran while one was open for 8% of the time, Pallas kernels for 18%

profile of v2, /device:TPU:12, one launch (start us, length us, event | category | flops | bytes accessed | tf_op | source)
XLA Modules:
  0.0 177.2 jit_solution(8201840822581186603)
XLA Ops:
  3.3 2.1 %dynamic-slice_bitcast_fusion.4 = bf16[4,2,64,1024]{3,1,0,2:T(2,128)(2,1)S(1)} fusion(bf16[64,4,2,4096]{3,2,1,0:T(2,128)(2,1)} %param.10, s32[]{:T(128)S(6)} %select_n.75), kind=kLoop, calls=%fused_computation.7 | loop fusion | bytes 2097156 | tf_op jit(solution)/shard_map/transpose | solution.py:360
  7.1 2.1 %collective-permute-start.3 = (bf16[1,2,64,1024]{3,2,1,0:T(8,128)(2,1)S(1)}, bf16[1,2,64,1024]{3,2,1,0:T(8,128)(2,1)S(1)}, u32[]{:S(2)}, u32[]{:S(2)}) collective-permute-start(bf16[1,2,64,1024]{3,2,1,0:T(8,128)(2,1)S(1)} %get-tuple-element.51), channel_id=1, source_target_pairs={{0,10},{2,8},{4,14},{6,12},{8,2},{10,0},{12,6},{14,4},{1,11},{3,9}... | collective-permute-start | bytes 786440 | tf_op jit(solution)/shard_map/ppermute | solution.py:350
  13.6 13.5 %collective-permute-done.3 = bf16[1,2,64,1024]{3,2,1,0:T(8,128)(2,1)S(1)} collective-permute-done((bf16[1,2,64,1024]{3,2,1,0:T(8,128)(2,1)S(1)}, bf16[1,2,64,1024]{3,2,1,0:T(8,128)(2,1)S(1)}, u32[]{:S(2)}, u32[]{:S(2)}) %collective-permute-start.3) | collective-permute-done | bytes 262176 | tf_op jit(solution)/shard_map/ppermute | solution.py:350
  27.1 5.6 %collective-permute-done.2 = bf16[1,2,64,1024]{3,2,1,0:T(8,128)(2,1)S(1)} collective-permute-done((bf16[1,2,64,1024]{3,2,1,0:T(8,128)(2,1)S(1)}, bf16[1,2,64,1024]{3,2,1,0:T(8,128)(2,1)S(1)}, u32[]{:S(2)}, u32[]{:S(2)}) %collective-permute-start.2) | collective-permute-done | bytes 262176 | tf_op jit(solution)/shard_map/ppermute | solution.py:350
  37.0 6.1 %dynamic-slice_bitcast_fusion.2 = (bf16[4,2,64,1024]{3,1,0,2:T(2,128)(2,1)S(1)}, bf16[4,2,64,1024]{3,1,0,2:T(2,128)(2,1)S(1)}, bf16[4,2,64,1024]{3,1,0,2:T(2,128)(2,1)S(1)}, bf16[4,2,64,1024]{3,1,0,2:T(2,128)(2,1)S(1)}) fusion(bf16[64,4,2,4096]{3,2,1,0:T(2,128)(2,1)} %param.10, s32[]{:T(128)S(6)} %select_n.84, s32[]{:T(128)S(6)} %select_n.94, ...), kind=kLoop, calls=%fused_computation.5 | loop fusion | bytes 8388624 | tf_op jit(solution)/shard_map/transpose | solution.py:360
  43.1 2.1 %slice_bitcast_fusion.19 = (bf16[2,64,1024]{2,0,1:T(2,128)(2,1)S(1)}, bf16[2,64,1024]{2,0,1:T(2,128)(2,1)S(1)}, bf16[2,64,1024]{2,0,1:T(2,128)(2,1)S(1)}, bf16[2...) fusion(bf16[4,2,64,1024]{3,1,0,2:T(2,128)(2,1)S(1)} %get-tuple-, ...), kind=kLoop, calls=%fused_computation.31 | loop fusion | bytes 4194304 | tf_op jit(solution)/shard_map/jit(_where)/broadcast_in_dim | solution.py:338
  45.9 2.1 %slice_bitcast_fusion.11 = (bf16[2,64,1024]{2,0,1:T(2,128)(2,1)S(1)}, bf16[2,64,1024]{2,0,1:T(2,128)(2,1)S(1)}, bf16[2,64,1024]{2,0,1:T(2,128)(2,1)S(1)}, bf16[2...) fusion(bf16[4,2,64,1024]{3,1,0,2:T(2,128)(2,1)S(1)} %get-tuple-, ...), kind=kLoop, calls=%fused_computation.23 | loop fusion | bytes 4194304 | tf_op jit(solution)/shard_map/jit(_where)/broadcast_in_dim | solution.py:338
  49.4 1.8 %collective-permute-start.4 = (bf16[1,2,64,1024]{3,2,1,0:T(8,128)(2,1)S(1)}, bf16[1,2,64,1024]{3,2,1,0:T(8,128)(2,1)S(1)}, u32[]{:S(2)}, u32[]{:S(2)}) collective-permute-start(bf16[1,2,64,1024]{3,2,1,0:T(8,128)(2,1)S(1)} %get-tuple-element.49), channel_id=1, source_target_pairs={{0,12},{2,14},{4,8},{6,10},{8,4},{10,6},{12,0},{14,2},{1,13},{3,15... | collective-permute-start | bytes 786440 | tf_op jit(solution)/shard_map/ppermute | solution.py:350
  51.4 9.0 %collective-permute-done.10.refs_8_ = bf16[4,2,64,1024]{3,2,1,0:T(8,128)(2,1)S(1)} collective-permute-done((bf16[4,2,64,1024]{3,2,1,0:T(8,128)(2,1)S(1)}, bf16[4,2,64,1024]{3,2,1,0:T(8,128)(2,1)S(1)}, u32[]{:S(2)}, u32[]{:S(2)}) %collective-permute-start.10) | collective-permute-done | bytes 1048608 | tf_op jit(solution)/shard_map/ppermute | solution.py:353
  63.6 6.2 %collective-permute-done.4 = bf16[1,2,64,1024]{3,2,1,0:T(8,128)(2,1)S(1)} collective-permute-done((bf16[1,2,64,1024]{3,2,1,0:T(8,128)(2,1)S(1)}, bf16[1,2,64,1024]{3,2,1,0:T(8,128)(2,1)S(1)}, u32[]{:S(2)}, u32[]{:S(2)}) %collective-permute-start.4) | collective-permute-done | bytes 262176 | tf_op jit(solution)/shard_map/ppermute | solution.py:350
  69.8 4.9 %collective-permute-done.5 = bf16[1,2,64,1024]{3,2,1,0:T(8,128)(2,1)S(1)} collective-permute-done((bf16[1,2,64,1024]{3,2,1,0:T(8,128)(2,1)S(1)}, bf16[1,2,64,1024]{3,2,1,0:T(8,128)(2,1)S(1)}, u32[]{:S(2)}, u32[]{:S(2)}) %collective-permute-start.5) | collective-permute-done | bytes 262176 | tf_op jit(solution)/shard_map/ppermute | solution.py:350
  78.5 20.9 %shard_map.113 = f32[6,2,64,1024]{3,2,1,0:T(8,128)} custom-call(s32[4]{0:T(128)S(1)} %iota_xor_fusion.order_ref, bf16[1,2,64,1024]{3,2,1,0:T(8,128)(2,1)S(1)} %get-tuple-element.87.refs_0_, bf16[1,2,64,1024]{3,2,1,0:T(8,128)(2,1)S(1)} %get-tuple-element.59.refs_1_, bf16[4,2,64,1024]{3,2,1,0:T(8,128)(2,1)} %copy-done, ...), custom_call_target="tpu_custom_call" | custom-call | flops 12884901888 | bytes 16777216 | tf_op jit(solution)/shard_map/pallas_call | solution.py:242
  99.5 2.2 %slice_bitcast_fusion.2 = (f32[2,64,1024]{2,1,0:T(8,128)S(1)}, f32[2,64,1024]{2,1,0:T(8,128)S(1)}, f32[2,64,1024]{2,1,0:T(8,128)S(1)}, f32[2,64,1024]{2,1,0:T(8,...) fusion(f32[6,2,64,1024]{3,2,1,0:T(8,128)} %shard_map.113), kind=kLoop, calls=%fused_computation.10 | loop fusion | bytes 6291456 | tf_op jit(solution)/shard_map/squeeze | solution.py:392
  103.0 1.6 collective-permute-start.14
  104.6 10.1 %shard_map.116.refs_2_ = f32[2,2,64,1024]{3,2,1,0:T(8,128)} custom-call(s32[3]{0:T(128)S(1)} %bitcast.96, bf16[2,2,64,1024]{3,2,1,0:T(8,128)(2,1)S(1)} %constant_dynamic-update-slice_fusion.refs_0_, bf16[2,2,64,1024]{3,2,1,0:T(8,128)(2,1)S(1)} %collective-permute-done.7.refs_1_, bf16[2,2,64,1024]{3,2,1,0:T(8,128)(2,1)S(1)} %collective-permute-done.6.refs_2_, ...), custom_call_target="tpu_custom_call" | custom-call | flops 3221225472 | bytes 12582912 | tf_op jit(solution)/shard_map/pallas_call | solution.py:242
  115.9 4.0 %shard_map.117 = f32[2,2,64,1024]{3,2,1,0:T(8,128)S(1)} custom-call(s32[1]{0:T(128)} %get-tuple-element.100.order_ref, bf16[1,2,64,1024]{3,2,1,0:T(8,128)(2,1)S(1)} %collective-permute-done.13.refs_0_, bf16[1,2,64,1024]{3,2,1,0:T(8,128)(2,1)S(1)} %collective-permute-done.14.refs_1_, f32[2,2,64,1024]{3,2,1,0:T(8,128)} %shard_map.116.refs_2_, ...), custom_call_target="tpu_custom_call" | custom-call | flops 1073741824 | bytes 4194304 | tf_op jit(solution)/shard_map/pallas_call | solution.py:242
  120.2 3.2 %collective-permute-start.20 = (s16[128,1152]{1,0:T(8,128)(2,1)S(1)}, s16[128,1152]{1,0:T(8,128)(2,1)S(1)}, u32[]{:S(2)}, u32[]{:S(2)}) collective-permute-start(s16[128,1152]{1,0:T(8,128)(2,1)S(1)} %shard_map.115), channel_id=1, source_target_pairs={{0,8},{2,10},{4,12},{6,14},{8,0},{10,2},{12,4},{14,6},{1,9},{3,11}... | collective-permute-start | bytes 884744 | tf_op jit(solution)/shard_map/ppermute | solution.py:350
  123.4 10.3 %collective-permute-done.19.refs_0_ = s16[128,1152]{1,0:T(8,128)(2,1)S(1)} collective-permute-done((s16[128,1152]{1,0:T(8,128)(2,1)S(1)}, s16[128,1152]{1,0:T(8,128)(2,1)S(1)}, u32[]{:S(2)}, u32[]{:S(2)}) %collective-permute-start.19) | collective-permute-done | bytes 294944 | tf_op jit(solution)/shard_map/ppermute | solution.py:350
  133.7 3.4 %collective-permute-done.20.refs_1_ = s16[128,1152]{1,0:T(8,128)(2,1)S(1)} collective-permute-done((s16[128,1152]{1,0:T(8,128)(2,1)S(1)}, s16[128,1152]{1,0:T(8,128)(2,1)S(1)}, u32[]{:S(2)}, u32[]{:S(2)}) %collective-permute-start.20) | collective-permute-done | bytes 294944 | tf_op jit(solution)/shard_map/ppermute | solution.py:350
  138.1 14.5 %collective-permute-done.21.refs_2_ = s16[128,1152]{1,0:T(8,128)(2,1)S(1)} collective-permute-done((s16[128,1152]{1,0:T(8,128)(2,1)S(1)}, s16[128,1152]{1,0:T(8,128)(2,1)S(1)}, u32[]{:S(2)}, u32[]{:S(2)}) %collective-permute-start.21) | collective-permute-done | bytes 294944 | tf_op jit(solution)/shard_map/ppermute | solution.py:350
  153.1 3.4 %collective-permute-start.22 = (f32[2,64,128]{2,1,0:T(8,128)S(1)}, f32[2,64,128]{2,1,0:T(8,128)S(1)}, u32[]{:S(2)}, u32[]{:S(2)}) collective-permute-start(f32[2,64,128]{2,1,0:T(8,128)S(1)} %get-tuple-element.34), channel_id=1, source_target_pairs={{0,1},{1,16},{16,17},{2,3},{3,18},{18,19},{4,5},{5,20},{20,21},{6,... | collective-permute-start | bytes 196616 | tf_op jit(solution)/shard_map/ppermute | solution.py:450
  156.5 2.5 %collective-permute-start.23 = (f32[2,64,128]{2,1,0:T(8,128)S(1)}, f32[2,64,128]{2,1,0:T(8,128)S(1)}, u32[]{:S(2)}, u32[]{:S(2)}) collective-permute-start(f32[2,64,128]{2,1,0:T(8,128)S(1)} %get-tuple-element.35), channel_id=1, source_target_pairs={{1,0},{16,1},{17,16},{3,2},{18,3},{19,18},{5,4},{20,5},{21,20},{7,... | collective-permute-start | bytes 196616 | tf_op jit(solution)/shard_map/ppermute | solution.py:451
  160.4 3.2 %collective-permute-done.23.high_ref = f32[2,64,128]{2,1,0:T(8,128)S(1)} collective-permute-done((f32[2,64,128]{2,1,0:T(8,128)S(1)}, f32[2,64,128]{2,1,0:T(8,128)S(1)}, u32[]{:S(2)}, u32[]{:S(2)}) %collective-permute-start.23) | collective-permute-done | bytes 65568 | tf_op jit(solution)/shard_map/ppermute | solution.py:451
  163.6 12.4 %shard_map.120 = f32[2,64,1024]{2,1,0:T(8,128)S(1)} custom-call(f32[2,64,128]{2,1,0:T(8,128)S(1)} %collective-permute-done.22.low_ref, f32[2,64,1024]{2,1,0:T(8,128)S(1)} %get-tuple-element.33.main_ref, f32[2,64,128]{2,1,0:T(8,128)S(1)} %collective-permute-done.23.high_ref, bf16[2,64,1024]{2,1,0:T(8,128)(2,1)S(1)} %bitcast.95, ...), custom_call_target="tpu_custom_call" | custom-call | tf_op jit(solution)/shard_map/pallas_call | solution.py:162
  (106 shorter events, 26.3 us)
Async XLA Ops:
  7.1 19.9 %collective-permute-start.3 = (bf16[1,2,64,1024]{3,2,1,0:T(8,128)(2,1)S(1)}, bf16[1,2,64,1024]{3,2,1,0:T(8,128)(2,1)S(1)}, u32[]{:S(2)}, u32[]{:S(2)}) collective-permute-start(bf16[1,2,64,1024]{3,2,1,0:T(8,128)(2,1)S(1)} %get-tuple-element.51), channel_id=1, source_target_pairs={{0,10},{2,8},{4,14},{6,12},{8,2},{10,0},{12,6},{14,4},{1,11},{3,9}... | collective-permute-start | bytes 786440 | tf_op jit(solution)/shard_map/ppermute | solution.py:350
  9.2 23.5 %collective-permute-start.2 = (bf16[1,2,64,1024]{3,2,1,0:T(8,128)(2,1)S(1)}, bf16[1,2,64,1024]{3,2,1,0:T(8,128)(2,1)S(1)}, u32[]{:S(2)}, u32[]{:S(2)}) collective-permute-start(bf16[1,2,64,1024]{3,2,1,0:T(8,128)(2,1)S(1)} %get-tuple-element.52), channel_id=1, source_target_pairs={{0,8},{2,10},{4,12},{6,14},{8,0},{10,2},{12,4},{14,6},{1,9},{3,11}... | collective-permute-start | bytes 786440 | tf_op jit(solution)/shard_map/ppermute | solution.py:350
  9.9 22.8 %collective-permute-start.1 = (bf16[1,2,64,1024]{3,2,1,0:T(8,128)(2,1)S(1)}, bf16[1,2,64,1024]{3,2,1,0:T(8,128)(2,1)S(1)}, u32[]{:S(2)}, u32[]{:S(2)}) collective-permute-start(bf16[1,2,64,1024]{3,2,1,0:T(8,128)(2,1)S(1)} %get-tuple-element.53), channel_id=1, source_target_pairs={{0,6},{2,4},{4,2},{6,0},{8,14},{10,12},{12,10},{14,8},{1,7},{3,5},... | collective-permute-start | bytes 786440 | tf_op jit(solution)/shard_map/ppermute | solution.py:350
  10.0 23.8 %collective-permute-start = (bf16[1,2,64,1024]{3,2,1,0:T(8,128)(2,1)S(1)}, bf16[1,2,64,1024]{3,2,1,0:T(8,128)(2,1)}, u32[]{:S(2)}, u32[]{:S(2)}) collective-permute-start(bf16[1,2,64,1024]{3,2,1,0:T(8,128)(2,1)S(1)} %get-tuple-element.50), channel_id=1, source_target_pairs={{0,4},{2,6},{4,0},{6,2},{8,12},{10,14},{12,8},{14,10},{1,5},{3,7},... | collective-permute-start | bytes 786440 | tf_op jit(solution)/shard_map/ppermute | solution.py:350
  34.9 27.1 %collective-permute-start.9 = (bf16[4,2,64,1024]{3,2,1,0:T(8,128)(2,1)S(1)}, bf16[4,2,64,1024]{3,2,1,0:T(8,128)(2,1)S(1)}, u32[]{:S(2)}, u32[]{:S(2)}) collective-permute-start(bf16[4,2,64,1024]{3,2,1,0:T(8,128)(2,1)S(1)} %pad_maximum_fusion.refs_2_), channel_id=1, source_target_pairs={{0,1},{1,0},{2,3},{3,2},{4,5},{5,4},{6,7},{7,6},{8,9},{9,8},{10,11... | collective-permute-start | bytes 3145736 | tf_op jit(solution)/shard_map/ppermute | solution.py:353
  35.5 24.9 %collective-permute-start.10 = (bf16[4,2,64,1024]{3,2,1,0:T(8,128)(2,1)S(1)}, bf16[4,2,64,1024]{3,2,1,0:T(8,128)(2,1)S(1)}, u32[]{:S(2)}, u32[]{:S(2)}) collective-permute-start(bf16[4,2,64,1024]{3,2,1,0:T(8,128)(2,1)S(1)} %pad_maximum_fusion.refs_2_), channel_id=1, source_target_pairs={{0,16},{16,0},{1,17},{17,1},{2,18},{18,2},{3,19},{19,3},{4,20},{20... | collective-permute-start | bytes 3145736 | tf_op jit(solution)/shard_map/ppermute | solution.py:353
  49.2 27.5 %collective-permute-start.8 = (bf16[4,2,64,1024]{3,2,1,0:T(8,128)(2,1)S(1)}, bf16[4,2,64,1024]{3,2,1,0:T(8,128)(2,1)S(1)}, u32[]{:S(2)}, u32[]{:S(2)}) collective-permute-start(bf16[4,2,64,1024]{3,2,1,0:T(8,128)(2,1)S(1)} %pad_maximum_fusion.1), channel_id=1, source_target_pairs={{0,2},{2,0},{4,6},{6,4},{8,10},{10,8},{12,14},{14,12},{1,3},{3,1},... | collective-permute-start | bytes 3145736 | tf_op jit(solution)/shard_map/ppermute | solution.py:350
  49.4 20.4 %collective-permute-start.4 = (bf16[1,2,64,1024]{3,2,1,0:T(8,128)(2,1)S(1)}, bf16[1,2,64,1024]{3,2,1,0:T(8,128)(2,1)S(1)}, u32[]{:S(2)}, u32[]{:S(2)}) collective-permute-start(bf16[1,2,64,1024]{3,2,1,0:T(8,128)(2,1)S(1)} %get-tuple-element.49), channel_id=1, source_target_pairs={{0,12},{2,14},{4,8},{6,10},{8,4},{10,6},{12,0},{14,2},{1,13},{3,15... | collective-permute-start | bytes 786440 | tf_op jit(solution)/shard_map/ppermute | solution.py:350
  51.2 23.5 %collective-permute-start.5 = (bf16[1,2,64,1024]{3,2,1,0:T(8,128)(2,1)S(1)}, bf16[1,2,64,1024]{3,2,1,0:T(8,128)(2,1)S(1)}, u32[]{:S(2)}, u32[]{:S(2)}) collective-permute-start(bf16[1,2,64,1024]{3,2,1,0:T(8,128)(2,1)S(1)} %get-tuple-element.48), channel_id=1, source_target_pairs={{0,14},{2,12},{4,10},{6,8},{8,6},{10,4},{12,2},{14,0},{1,15},{3,13... | collective-permute-start | bytes 786440 | tf_op jit(solution)/shard_map/ppermute | solution.py:350
  60.4 17.2 %collective-permute-start.11 = (bf16[2,2,64,1024]{3,2,1,0:T(8,128)(2,1)S(1)}, bf16[2,2,64,1024]{3,2,1,0:T(8,128)(2,1)S(1)}, u32[]{:S(2)}, u32[]{:S(2)}) collective-permute-start(bf16[2,2,64,1024]{3,2,1,0:T(8,128)(2,1)S(1)} %slice.349), channel_id=1, source_target_pairs={{0,1},{1,0},{2,3},{3,2},{4,5},{5,4},{6,7},{7,6},{8,9},{9,8},{10,11... | collective-permute-start | bytes 1572872 | tf_op jit(solution)/shard_map/ppermute | solution.py:353
  62.0 15.6 %collective-permute-start.12 = (bf16[2,2,64,1024]{3,2,1,0:T(8,128)(2,1)S(1)}, bf16[2,2,64,1024]{3,2,1,0:T(8,128)(2,1)S(1)}, u32[]{:S(2)}, u32[]{:S(2)}) collective-permute-start(bf16[2,2,64,1024]{3,2,1,0:T(8,128)(2,1)S(1)} %slice.350), channel_id=1, source_target_pairs={{0,16},{16,0},{1,17},{17,1},{2,18},{18,2},{3,19},{19,3},{4,20},{20... | collective-permute-start | bytes 1572872 | tf_op jit(solution)/shard_map/ppermute | solution.py:353
  74.7 24.8 %collective-permute-start.6 = (bf16[2,2,64,1024]{3,2,1,0:T(8,128)(2,1)S(1)}, bf16[2,2,64,1024]{3,2,1,0:T(8,128)(2,1)S(1)}, u32[]{:S(2)}, u32[]{:S(2)}) collective-permute-start(bf16[2,2,64,1024]{3,2,1,0:T(8,128)(2,1)S(1)} %constant_dynamic-update-slice_fusion.refs_0_), channel_id=1, source_target_pairs={{0,16},{16,0},{1,17},{17,1},{2,18},{18,2},{3,19},{19,3},{4,20},{20... | collective-permute-start | bytes 1572872 | tf_op jit(solution)/shard_map/ppermute | solution.py:353
  75.3 24.2 %collective-permute-start.7 = (bf16[2,2,64,1024]{3,2,1,0:T(8,128)(2,1)S(1)}, bf16[2,2,64,1024]{3,2,1,0:T(8,128)(2,1)S(1)}, u32[]{:S(2)}, u32[]{:S(2)}) collective-permute-start(bf16[2,2,64,1024]{3,2,1,0:T(8,128)(2,1)S(1)} %constant_dynamic-update-slice_fusion.refs_0_), channel_id=1, source_target_pairs={{0,1},{1,0},{2,3},{3,2},{4,5},{5,4},{6,7},{7,6},{8,9},{9,8},{10,11... | collective-permute-start | bytes 1572872 | tf_op jit(solution)/shard_map/ppermute | solution.py:353
  101.7 13.0 %collective-permute-start.15 = (f32[2,64,1024]{2,1,0:T(8,128)S(1)}, f32[2,64,1024]{2,1,0:T(8,128)S(1)}, u32[]{:S(2)}, u32[]{:S(2)}) collective-permute-start(f32[2,64,1024]{2,1,0:T(8,128)S(1)} %get-tuple-element.45), channel_id=1, source_target_pairs={{0,2},{2,0},{4,6},{6,4},{8,10},{10,8},{12,14},{14,12},{1,3},{3,1},... | collective-permute-start | bytes 1572872 | tf_op jit(solution)/shard_map/ppermute | solution.py:350
  101.8 13.5 %collective-permute-start.16 = (f32[2,64,1024]{2,1,0:T(8,128)S(1)}, f32[2,64,1024]{2,1,0:T(8,128)S(1)}, u32[]{:S(2)}, u32[]{:S(2)}) collective-permute-start(f32[2,64,1024]{2,1,0:T(8,128)S(1)} %get-tuple-element.43), channel_id=1, source_target_pairs={{0,2},{2,0},{4,6},{6,4},{8,10},{10,8},{12,14},{14,12},{1,3},{3,1},... | collective-permute-start | bytes 1572872 | tf_op jit(solution)/shard_map/ppermute | solution.py:350
  102.3 13.6 %collective-permute-start.17 = (f32[2,64,1024]{2,1,0:T(8,128)S(1)}, f32[2,64,1024]{2,1,0:T(8,128)S(1)}, u32[]{:S(2)}, u32[]{:S(2)}) collective-permute-start(f32[2,64,1024]{2,1,0:T(8,128)S(1)} %get-tuple-element.42), channel_id=1, source_target_pairs={{0,2},{2,0},{4,6},{6,4},{8,10},{10,8},{12,14},{14,12},{1,3},{3,1},... | collective-permute-start | bytes 1572872 | tf_op jit(solution)/shard_map/ppermute | solution.py:350
  102.4 13.5 %collective-permute-start.13 = (bf16[1,2,64,1024]{3,2,1,0:T(8,128)(2,1)S(1)}, bf16[1,2,64,1024]{3,2,1,0:T(8,128)(2,1)S(1)}, u32[]{:S(2)}, u32[]{:S(2)}) collective-permute-start(bf16[1,2,64,1024]{3,2,1,0:T(8,128)(2,1)S(1)} %slice.295), channel_id=1, source_target_pairs={{0,1},{1,0},{2,3},{3,2},{4,5},{5,4},{6,7},{7,6},{8,9},{9,8},{10,11... | collective-permute-start | bytes 786440 | tf_op jit(solution)/shard_map/ppermute | solution.py:353
  103.0 12.9 %collective-permute-start.14 = (bf16[1,2,64,1024]{3,2,1,0:T(8,128)(2,1)S(1)}, bf16[1,2,64,1024]{3,2,1,0:T(8,128)(2,1)S(1)}, u32[]{:S(2)}, u32[]{:S(2)}) collective-permute-start(bf16[1,2,64,1024]{3,2,1,0:T(8,128)(2,1)S(1)} %slice.296), channel_id=1, source_target_pairs={{0,16},{16,0},{1,17},{17,1},{2,18},{18,2},{3,19},{19,3},{4,20},{20... | collective-permute-start | bytes 786440 | tf_op jit(solution)/shard_map/ppermute | solution.py:353
  120.0 17.1 %collective-permute-start.18 = (f32[2,64,1024]{2,1,0:T(8,128)S(1)}, f32[2,64,1024]{2,1,0:T(8,128)S(1)}, u32[]{:S(2)}, u32[]{:S(2)}) collective-permute-start(f32[2,64,1024]{2,1,0:T(8,128)S(1)} %get-tuple-element.55), channel_id=1, source_target_pairs={{0,2},{2,0},{4,6},{6,4},{8,10},{10,8},{12,14},{14,12},{1,3},{3,1},... | collective-permute-start | bytes 1572872 | tf_op jit(solution)/shard_map/ppermute | solution.py:350
  120.1 13.5 %collective-permute-start.19 = (s16[128,1152]{1,0:T(8,128)(2,1)S(1)}, s16[128,1152]{1,0:T(8,128)(2,1)S(1)}, u32[]{:S(2)}, u32[]{:S(2)}) collective-permute-start(s16[128,1152]{1,0:T(8,128)(2,1)S(1)} %shard_map.114), channel_id=1, source_target_pairs={{0,4},{2,6},{4,0},{6,2},{8,12},{10,14},{12,8},{14,10},{1,5},{3,7},... | collective-permute-start | bytes 884744 | tf_op jit(solution)/shard_map/ppermute | solution.py:350
  120.2 16.9 %collective-permute-start.20 = (s16[128,1152]{1,0:T(8,128)(2,1)S(1)}, s16[128,1152]{1,0:T(8,128)(2,1)S(1)}, u32[]{:S(2)}, u32[]{:S(2)}) collective-permute-start(s16[128,1152]{1,0:T(8,128)(2,1)S(1)} %shard_map.115), channel_id=1, source_target_pairs={{0,8},{2,10},{4,12},{6,14},{8,0},{10,2},{12,4},{14,6},{1,9},{3,11}... | collective-permute-start | bytes 884744 | tf_op jit(solution)/shard_map/ppermute | solution.py:350
  137.7 14.9 %collective-permute-start.21 = (s16[128,1152]{1,0:T(8,128)(2,1)S(1)}, s16[128,1152]{1,0:T(8,128)(2,1)S(1)}, u32[]{:S(2)}, u32[]{:S(2)}) collective-permute-start(s16[128,1152]{1,0:T(8,128)(2,1)S(1)} %shard_map.118), channel_id=1, source_target_pairs={{0,12},{2,14},{4,8},{6,10},{8,4},{10,6},{12,0},{14,2},{1,13},{3,15... | collective-permute-start | bytes 884744 | tf_op jit(solution)/shard_map/ppermute | solution.py:350
  153.1 7.2 %collective-permute-start.22 = (f32[2,64,128]{2,1,0:T(8,128)S(1)}, f32[2,64,128]{2,1,0:T(8,128)S(1)}, u32[]{:S(2)}, u32[]{:S(2)}) collective-permute-start(f32[2,64,128]{2,1,0:T(8,128)S(1)} %get-tuple-element.34), channel_id=1, source_target_pairs={{0,1},{1,16},{16,17},{2,3},{3,18},{18,19},{4,5},{5,20},{20,21},{6,... | collective-permute-start | bytes 196616 | tf_op jit(solution)/shard_map/ppermute | solution.py:450
  156.5 7.1 %collective-permute-start.23 = (f32[2,64,128]{2,1,0:T(8,128)S(1)}, f32[2,64,128]{2,1,0:T(8,128)S(1)}, u32[]{:S(2)}, u32[]{:S(2)}) collective-permute-start(f32[2,64,128]{2,1,0:T(8,128)S(1)} %get-tuple-element.35), channel_id=1, source_target_pairs={{1,0},{16,1},{17,16},{3,2},{18,3},{19,18},{5,4},{20,5},{21,20},{7,... | collective-permute-start | bytes 196616 | tf_op jit(solution)/shard_map/ppermute | solution.py:451
  (8 other events, 88.3 us)

commit v3 on v2

--- a/solution.py
+++ b/solution.py
@@ -176,9 +176,9 @@
     )(low, main, high, rec, lanes_shift)
 
 
-def product_kernel(order_ref, *refs, layout, has_base):
-    panel_ref, out_ref, by_real, by_imag = refs[-4:]
-    groups, comps, shots, width = out_ref.shape
+def product_kernel(order_ref, *refs, layout):
+    panel_ref, keep_ref, swap_ref, by_real, by_imag = refs[-5:]
+    pairs, comps, shots, width = keep_ref.shape
     step = pl.program_id(1)
     real, imag = panel_ref[0], panel_ref[1]
 
@@ -201,18 +201,16 @@
 
     @pl.when(step == pl.num_programs(1) - 1)
     def _():
-        for g in range(groups):
+        for g in range(2 * pairs):
             row = 2 * g * shots
             real_part = by_real[row : row + shots] - by_imag[row + shots : row + 2 * shots]
             imag_part = by_imag[row : row + shots] + by_real[row + shots : row + 2 * shots]
-            if has_base:
-                real_part += refs[at][g, 0]
-                imag_part += refs[at][g, 1]
-            out_ref[g, 0] = real_part
-            out_ref[g, 1] = imag_part
-
-
-def products(pieces, order, panel, depth, base=None):
+            out_ref = swap_ref if g % 2 else keep_ref
+            out_ref[g // 2, 0] = real_part
+            out_ref[g // 2, 1] = imag_part
+
+
+def products(pieces, order, panel, depth):
     _, comps, _, width = panel.shape
     parts = len(pieces)
     tile = width // 2
@@ -227,26 +225,22 @@
             specs.append(
                 pl.BlockSpec(piece.shape[:3] + (depth,), lambda n, k, o, block=block: (0, 0, 0, block))
             )
-    out_spec = pl.BlockSpec((groups, comps, shots, tile), lambda n, k, o: (0, 0, 0, n))
-    if base is not None:
-        flat.append(base)
-        specs.append(out_spec)
+    out_spec = pl.BlockSpec((groups // 2, comps, shots, tile), lambda n, k, o: (0, 0, 0, n))
     grid_spec = pltpu.PrefetchScalarGridSpec(
         num_scalar_prefetch=1,
         grid=(width // tile, parts),
         in_specs=specs
         + [pl.BlockSpec((None, comps, depth, tile), lambda n, k, o: (0, 0, o[k], n))],
-        out_specs=out_spec,
+        out_specs=(out_spec, out_spec),
         scratch_shapes=[pltpu.VMEM((rows, tile), jnp.float32)] * 2,
     )
     return pl.pallas_call(
         functools.partial(
             product_kernel,
             layout=tuple(len(part) for part in pieces),
-            has_base=base is not None,
         ),
         grid_spec=grid_spec,
-        out_shape=jax.ShapeDtypeStruct((groups, comps, shots, width), jnp.float32),
+        out_shape=(jax.ShapeDtypeStruct((groups // 2, comps, shots, width), jnp.float32),) * 2,
         compiler_params=pltpu.CompilerParams(vmem_limit_bytes=52 * 1024 * 1024),
         cost_estimate=pl.CostEstimate(
             flops=4 * rows * depth * parts * width,
@@ -284,13 +278,18 @@
         out_ref[rows, width:] = power.astype(jnp.int32).astype(jnp.int16)
 
 
-def coded(first, second):
-    comps, shots, width = first.shape
+def pair_spec(array, pair):
+    return pl.BlockSpec((None,) + array.shape[1:], lambda i: (pair, 0, 0, 0))
+
+
+def coded(first, second, pair):
+    _, comps, shots, width = first.shape
     return pl.pallas_call(
         code_kernel,
+        grid=(1,),
         out_shape=jax.ShapeDtypeStruct((comps * shots, width + LANES), jnp.int16),
-        in_specs=[pl.BlockSpec(memory_space=pltpu.VMEM)] * 2,
-        out_specs=pl.BlockSpec(memory_space=pltpu.VMEM),
+        in_specs=[pair_spec(first, pair), pair_spec(second, pair)],
+        out_specs=pl.BlockSpec((comps * shots, width + LANES), lambda i: (0, 0)),
         compiler_params=pltpu.CompilerParams(vmem_limit_bytes=16 * 1024 * 1024),
     )(first, second)
 
@@ -320,13 +319,16 @@
 
 
 def summed(first, second, codes):
-    comps, shots, width = first.shape
+    _, comps, shots, width = first.shape
     end = jax.ShapeDtypeStruct((comps, shots, LANES), jnp.float32)
     return pl.pallas_call(
         sum_kernel,
-        out_shape=(jax.ShapeDtypeStruct(first.shape, jnp.float32), end, end),
-        in_specs=[pl.BlockSpec(memory_space=pltpu.VMEM)] * (2 + len(codes)),
-        out_specs=(pl.BlockSpec(memory_space=pltpu.VMEM),) * 3,
+        grid=(1,),
+        out_shape=(jax.ShapeDtypeStruct(first.shape[1:], jnp.float32), end, end),
+        in_specs=[pair_spec(first, 0), pair_spec(second, 0)]
+        + [pl.BlockSpec(code.shape, lambda i: (0, 0)) for code in codes],
+        out_specs=(pl.BlockSpec(first.shape[1:], lambda i: (0, 0, 0)),)
+        + (pl.BlockSpec(end.shape, lambda i: (0, 0, 0)),) * 2,
         compiler_params=pltpu.CompilerParams(vmem_limit_bytes=16 * 1024 * 1024),
     )(first, second, *codes)
 
@@ -384,21 +386,22 @@
     lists = [
         (local[n][:1], sibling[0][n : n + 1]) + tuple(exchanged[n]) for n in range(parts)
     ]
-    terms = products(lists, order, panel, depth)
-    late_sec, late_win, terms = fence((late_sec, late_win, terms))
+    keep, swap = products(lists, order, panel, depth)
+    late_sec, late_win, keep, swap = fence((late_sec, late_win, keep, swap))
     half = len(late) // 2
     late_both = (across(late_sec[:half], "win"), across(late_win[half:], "sec"))
-    most = products(((own_late,), (late_win,), (late_sec,)), order[:3], panel, depth)
-    others = [partner(terms[n + 1], 1) for n in range(0, 2 + len(early), 2)]
-    codes = [coded(terms[2 * n], others[n]) for n in range(1, 1 + len(early) // 2)]
-    late_both, codes, others = fence((late_both, codes, others))
-    last = products((late_both,), order[3:], panel, depth, most)
+    swap = partner(swap, 1)
+    codes = [coded(keep, swap, n) for n in range(1, 1 + len(early) // 2)]
+    late_both, codes, swap = fence((late_both, codes, swap))
+    last, late_swap = products(
+        ((own_late,), (late_win,), (late_sec,), late_both), order, panel, depth
+    )
     codes = [partner(code, k) for code, k in zip(codes, early[::2])]
-    late_others = [partner(last[n + 1], 1) for n in range(0, len(late), 2)]
-    late_others, codes = fence((late_others, codes))
+    late_swap, codes = fence((late_swap, codes))
+    late_swap = partner(late_swap, 1)
     for n, k in enumerate(late[::2]):
-        codes.append(partner(coded(last[2 * n], late_others[n]), k))
-    return summed(terms[0], others[0], codes)
+        codes.append(partner(coded(last, late_swap, n), k))
+    return summed(keep, swap, codes)
 
 
 def predict_slots(shot_rows, aperture, panel, capacity):

time: 178 us -> 169 us (0.949)
  waiting for transfers between devices: 71.7 us -> 65.4 us
    ppermute x14 -> x12, waiting for transfers between devices: 59.5 us -> 49.8 us  [partner(): lax.ppermute(value, 'shot', [(i, i ^ step) for i in range(panel_count)])]
    ppermute x8, waiting for transfers between devices: 8.98 us -> 11.9 us  [across(): return lax.ppermute(value, axis, [(0, 1), (1, 0)])]
    squeeze x2 -> x0, local copies, waits for them, and re-layouts: 2.34 us -> none  [the longest x1 2.24 us: predict_dense(): others = [partner(terms[n + 1], 1) for n in range(0, 2 + len(early), 2)]]
    pallas_call x3 -> x2, Pallas kernels: 35 us -> 33.4 us  [products(): pl.pallas_call(functools.partial(product_kernel, layout=tuple((len(part)...]
    unnamed x20 -> x30, local copies, waits for them, and re-layouts: 3.44 us -> 4.87 us
    ppermute x14 -> x12, starting transfers between devices: 10.9 us -> 10.2 us  [partner(): lax.ppermute(value, 'shot', [(i, i ^ step) for i in range(panel_count)])]
  transfers between devices with their start and end apart: 24 -> 22, of which waited for: 10 -> 13; matrix products, arithmetic and copies ran while one was open for 8% -> 9% of each run, Pallas kernels for 18% -> 21%
where the time goes in v3:
time: 169 us; the launch traced here: 168 us
  waiting for transfers between devices  65.4 us (39%)
  Pallas kernels  48.1 us (28%)
  starting transfers between devices  25.9 us (15%)
  local copies, waits for them, and re-layouts  20.9 us (12%)
  other arithmetic  4.04 us (2%)
  between operations  3.81 us (2%)
    ppermute x12, waiting for transfers between devices, partner(): lax.ppermute(value, 'shot', [(i, i ^ step) for i in range(panel_count)])  49.8 us
    pallas_call x2, Pallas kernels, products(): pl.pallas_call(functools.partial(product_kernel, layout=tuple((len(part)...  33.4 us
    pallas_call x1, Pallas kernels, fit(): pl.pallas_call(fit_kernel, out_shape=jax.ShapeDtypeStruct(main.shape, jnp...  12.4 us
    ppermute x8, waiting for transfers between devices, across(): return lax.ppermute(value, axis, [(0, 1), (1, 0)])  11.9 us
    ppermute x12, starting transfers between devices, partner(): lax.ppermute(value, 'shot', [(i, i ^ step) for i in range(panel_count)])  10.2 us
    ppermute x8, starting transfers between devices, across(): return lax.ppermute(value, axis, [(0, 1), (1, 0)])  9.45 us
    transpose x2, local copies, waits for them, and re-layouts, turned(): return here.transpose(1, 2, 0, 3)  8.25 us
    broadcast_in_dim x25, local copies, waits for them, and re-layouts, chosen(): out = jnp.where(named[:, a, None, :, None], rows[a][None], out)  5.87 us
  transfers between devices with their start and end apart: 22, of which 13 were waited for; matrix products, arithmetic and copies ran while one was open for 9% of the time, Pallas kernels for 21%

profile of v3, /device:TPU:12, one launch (start us, length us, event | category | flops | bytes accessed | tf_op | source)
XLA Modules:
  0.0 168.2 jit_solution(15232848240984239656)
XLA Ops:
  3.4 2.1 %dynamic-slice_bitcast_fusion.4 = bf16[4,2,64,1024]{3,1,0,2:T(2,128)(2,1)S(1)} fusion(bf16[64,4,2,4096]{3,2,1,0:T(2,128)(2,1)} %param.10, s32[]{:T(128)S(6)} %select_n.75), kind=kLoop, calls=%fused_computation.7 | loop fusion | bytes 2097156 | tf_op jit(solution)/shard_map/transpose | solution.py:362
  7.1 2.1 %collective-permute-start.3 = (bf16[1,2,64,1024]{3,2,1,0:T(8,128)(2,1)S(1)}, bf16[1,2,64,1024]{3,2,1,0:T(8,128)(2,1)S(1)}, u32[]{:S(2)}, u32[]{:S(2)}) collective-permute-start(bf16[1,2,64,1024]{3,2,1,0:T(8,128)(2,1)S(1)} %get-tuple-element.55), channel_id=1, source_target_pairs={{0,10},{2,8},{4,14},{6,12},{8,2},{10,0},{12,6},{14,4},{1,11},{3,9}... | collective-permute-start | bytes 786440 | tf_op jit(solution)/shard_map/ppermute | solution.py:352
  10.0 1.6 collective-permute-start
  13.7 13.4 %collective-permute-done.3 = bf16[1,2,64,1024]{3,2,1,0:T(8,128)(2,1)S(1)} collective-permute-done((bf16[1,2,64,1024]{3,2,1,0:T(8,128)(2,1)S(1)}, bf16[1,2,64,1024]{3,2,1,0:T(8,128)(2,1)S(1)}, u32[]{:S(2)}, u32[]{:S(2)}) %collective-permute-start.3) | collective-permute-done | bytes 262176 | tf_op jit(solution)/shard_map/ppermute | solution.py:352
  27.1 5.6 %collective-permute-done.2 = bf16[1,2,64,1024]{3,2,1,0:T(8,128)(2,1)S(1)} collective-permute-done((bf16[1,2,64,1024]{3,2,1,0:T(8,128)(2,1)S(1)}, bf16[1,2,64,1024]{3,2,1,0:T(8,128)(2,1)S(1)}, u32[]{:S(2)}, u32[]{:S(2)}) %collective-permute-start.2) | collective-permute-done | bytes 262176 | tf_op jit(solution)/shard_map/ppermute | solution.py:352
  37.0 6.1 %dynamic-slice_bitcast_fusion.2 = (bf16[4,2,64,1024]{3,1,0,2:T(2,128)(2,1)S(1)}, bf16[4,2,64,1024]{3,1,0,2:T(2,128)(2,1)S(1)}, bf16[4,2,64,1024]{3,1,0,2:T(2,128)(2,1)S(1)}, bf16[4,2,64,1024]{3,1,0,2:T(2,128)(2,1)S(1)}) fusion(bf16[64,4,2,4096]{3,2,1,0:T(2,128)(2,1)} %param.10, s32[]{:T(128)S(6)} %select_n.84, s32[]{:T(128)S(6)} %select_n.94, ...), kind=kLoop, calls=%fused_computation.5 | loop fusion | bytes 8388624 | tf_op jit(solution)/shard_map/transpose | solution.py:362
  43.1 2.1 %slice_bitcast_fusion.11 = (bf16[2,64,1024]{2,0,1:T(2,128)(2,1)S(1)}, bf16[2,64,1024]{2,0,1:T(2,128)(2,1)S(1)}, bf16[2,64,1024]{2,0,1:T(2,128)(2,1)S(1)}, bf16[2...) fusion(bf16[4,2,64,1024]{3,1,0,2:T(2,128)(2,1)S(1)} %get-tuple-, ...), kind=kLoop, calls=%fused_computation.23 | loop fusion | bytes 4194304 | tf_op jit(solution)/shard_map/jit(_where)/broadcast_in_dim | solution.py:340
  46.0 2.1 %slice_bitcast_fusion.3 = (bf16[2,64,1024]{2,0,1:T(2,128)(2,1)S(1)}, bf16[2,64,1024]{2,0,1:T(2,128)(2,1)S(1)}, bf16[2,64,1024]{2,0,1:T(2,128)(2,1)S(1)}, bf16[2,...) fusion(bf16[4,2,64,1024]{3,1,0,2:T(2,128)(2,1)S(1)} %get-tuple-, ...), kind=kLoop, calls=%fused_computation.15 | loop fusion | bytes 4194304 | tf_op jit(solution)/shard_map/jit(_where)/broadcast_in_dim | solution.py:340
  49.4 1.8 %collective-permute-start.4 = (bf16[1,2,64,1024]{3,2,1,0:T(8,128)(2,1)S(1)}, bf16[1,2,64,1024]{3,2,1,0:T(8,128)(2,1)S(1)}, u32[]{:S(2)}, u32[]{:S(2)}) collective-permute-start(bf16[1,2,64,1024]{3,2,1,0:T(8,128)(2,1)S(1)} %get-tuple-element.53), channel_id=1, source_target_pairs={{0,12},{2,14},{4,8},{6,10},{8,4},{10,6},{12,0},{14,2},{1,13},{3,15... | collective-permute-start | bytes 786440 | tf_op jit(solution)/shard_map/ppermute | solution.py:352
  51.4 9.0 %collective-permute-done.10.refs_8_ = bf16[4,2,64,1024]{3,2,1,0:T(8,128)(2,1)S(1)} collective-permute-done((bf16[4,2,64,1024]{3,2,1,0:T(8,128)(2,1)S(1)}, bf16[4,2,64,1024]{3,2,1,0:T(8,128)(2,1)S(1)}, u32[]{:S(2)}, u32[]{:S(2)}) %collective-permute-start.10) | collective-permute-done | bytes 1048608 | tf_op jit(solution)/shard_map/ppermute | solution.py:355
  60.4 1.6 collective-permute-start.11
  63.6 6.2 %collective-permute-done.4 = bf16[1,2,64,1024]{3,2,1,0:T(8,128)(2,1)S(1)} collective-permute-done((bf16[1,2,64,1024]{3,2,1,0:T(8,128)(2,1)S(1)}, bf16[1,2,64,1024]{3,2,1,0:T(8,128)(2,1)S(1)}, u32[]{:S(2)}, u32[]{:S(2)}) %collective-permute-start.4) | collective-permute-done | bytes 262176 | tf_op jit(solution)/shard_map/ppermute | solution.py:352
  69.8 4.9 %collective-permute-done.5 = bf16[1,2,64,1024]{3,2,1,0:T(8,128)(2,1)S(1)} collective-permute-done((bf16[1,2,64,1024]{3,2,1,0:T(8,128)(2,1)S(1)}, bf16[1,2,64,1024]{3,2,1,0:T(8,128)(2,1)S(1)}, u32[]{:S(2)}, u32[]{:S(2)}) %collective-permute-start.5) | collective-permute-done | bytes 262176 | tf_op jit(solution)/shard_map/ppermute | solution.py:352
  78.6 20.9 %shard_map.113 = (f32[3,2,64,1024]{3,2,1,0:T(8,128)}, f32[3,2,64,1024]{3,2,1,0:T(8,128)}) custom-call(s32[4]{0:T(128)S(1)} %iota_xor_fusion.order_ref, bf16[1,2,64,1024]{3,2,1,0:T(8,128)(2,1)S(1)} %get-tuple-element.89.refs_0_, bf16[1,2,64,1024]{3,2,1,0:T(8,128)(2,1)S(1)} %get-tuple-element.61.refs_1_, bf16[4,2,64,1024]{3,2,1,0:T(8,128)(2,1)} %copy-done.5, ...), custom_call_target="tpu_custom_call" | custom-call | flops 12884901888 | bytes 16777216 | tf_op jit(solution)/shard_map/pallas_call | solution.py:237
  100.2 1.6 collective-permute-start.14
  105.8 2.6 %collective-permute-done.13.refs_3_ = bf16[1,2,64,1024]{3,2,1,0:T(8,128)(2,1)S(1)} collective-permute-done((bf16[1,2,64,1024]{3,2,1,0:T(8,128)(2,1)S(1)}, bf16[1,2,64,1024]{3,2,1,0:T(8,128)(2,1)S(1)}, u32[]{:S(2)}, u32[]{:S(2)}) %collective-permute-start.13) | collective-permute-done | bytes 262176 | tf_op jit(solution)/shard_map/ppermute | solution.py:355
  108.7 3.1 %collective-permute-start.17 = (s16[128,1152]{1,0:T(8,128)(2,1)S(1)}, s16[128,1152]{1,0:T(8,128)(2,1)S(1)}, u32[]{:S(2)}, u32[]{:S(2)}) collective-permute-start(s16[128,1152]{1,0:T(8,128)(2,1)S(1)} %shard_map.115), channel_id=1, source_target_pairs={{0,8},{2,10},{4,12},{6,14},{8,0},{10,2},{12,4},{14,6},{1,9},{3,11}... | collective-permute-start | bytes 884744 | tf_op jit(solution)/shard_map/ppermute | solution.py:352
  111.9 12.4 %shard_map.116 = (f32[1,2,64,1024]{3,2,1,0:T(8,128)S(1)}, f32[1,2,64,1024]{3,2,1,0:T(8,128)S(1)}) custom-call(s32[4]{0:T(128)S(1)} %iota_xor_fusion.order_ref, bf16[2,2,64,1024]{3,2,1,0:T(8,128)(2,1)} %copy-done.4, bf16[2,2,64,1024]{3,2,1,0:T(8,128)(2,1)} %copy-done.3, bf16[2,2,64,1024]{3,2,1,0:T(8,128)(2,1)} %copy-done.2, ...), custom_call_target="tpu_custom_call" | custom-call | flops 4294967296 | bytes 16777216 | tf_op jit(solution)/shard_map/pallas_call | solution.py:237
  124.6 1.9 %collective-permute-done.18.second_ref = f32[1,2,64,1024]{3,2,1,0:T(8,128)S(1)} collective-permute-done((f32[1,2,64,1024]{3,2,1,0:T(8,128)S(1)}, f32[1,2,64,1024]{3,2,1,0:T(8,128)S(1)}, u32[]{:S(2)}, u32[]{:S(2)}) %collective-permute-start.18) | collective-permute-done | bytes 524320 | tf_op jit(solution)/shard_map/ppermute | solution.py:352
  127.5 15.0 %collective-permute-done.19.refs_2_ = s16[128,1152]{1,0:T(8,128)(2,1)S(1)} collective-permute-done((s16[128,1152]{1,0:T(8,128)(2,1)S(1)}, s16[128,1152]{1,0:T(8,128)(2,1)S(1)}, u32[]{:S(2)}, u32[]{:S(2)}) %collective-permute-start.19) | collective-permute-done | bytes 294944 | tf_op jit(solution)/shard_map/ppermute | solution.py:352
  143.1 4.4 %collective-permute-start.20 = (f32[2,64,128]{2,1,0:T(8,128)S(1)}, f32[2,64,128]{2,1,0:T(8,128)S(1)}, u32[]{:S(2)}, u32[]{:S(2)}) collective-permute-start(f32[2,64,128]{2,1,0:T(8,128)S(1)} %get-tuple-element.44), channel_id=1, source_target_pairs={{0,1},{1,16},{16,17},{2,3},{3,18},{18,19},{4,5},{5,20},{20,21},{6,... | collective-permute-start | bytes 196616 | tf_op jit(solution)/shard_map/ppermute | solution.py:453
  147.5 1.9 %collective-permute-start.21 = (f32[2,64,128]{2,1,0:T(8,128)S(1)}, f32[2,64,128]{2,1,0:T(8,128)S(1)}, u32[]{:S(2)}, u32[]{:S(2)}) collective-permute-start(f32[2,64,128]{2,1,0:T(8,128)S(1)} %get-tuple-element.45), channel_id=1, source_target_pairs={{1,0},{16,1},{17,16},{3,2},{18,3},{19,18},{5,4},{20,5},{21,20},{7,... | collective-permute-start | bytes 196616 | tf_op jit(solution)/shard_map/ppermute | solution.py:454
  150.8 3.8 %collective-permute-done.21.high_ref = f32[2,64,128]{2,1,0:T(8,128)S(1)} collective-permute-done((f32[2,64,128]{2,1,0:T(8,128)S(1)}, f32[2,64,128]{2,1,0:T(8,128)S(1)}, u32[]{:S(2)}, u32[]{:S(2)}) %collective-permute-start.21) | collective-permute-done | bytes 65568 | tf_op jit(solution)/shard_map/ppermute | solution.py:454
  154.5 12.4 %shard_map.119 = f32[2,64,1024]{2,1,0:T(8,128)S(1)} custom-call(f32[2,64,128]{2,1,0:T(8,128)S(1)} %collective-permute-done.20.low_ref, f32[2,64,1024]{2,1,0:T(8,128)S(1)} %get-tuple-element.43.main_ref, f32[2,64,128]{2,1,0:T(8,128)S(1)} %collective-permute-done.21.high_ref, bf16[2,64,1024]{2,1,0:T(8,128)(2,1)S(1)} %bitcast.78, ...), custom_call_target="tpu_custom_call" | custom-call | tf_op jit(solution)/shard_map/pallas_call | solution.py:162
  (109 shorter events, 25.7 us)
Async XLA Ops:
  7.1 19.9 %collective-permute-start.3 = (bf16[1,2,64,1024]{3,2,1,0:T(8,128)(2,1)S(1)}, bf16[1,2,64,1024]{3,2,1,0:T(8,128)(2,1)S(1)}, u32[]{:S(2)}, u32[]{:S(2)}) collective-permute-start(bf16[1,2,64,1024]{3,2,1,0:T(8,128)(2,1)S(1)} %get-tuple-element.55), channel_id=1, source_target_pairs={{0,10},{2,8},{4,14},{6,12},{8,2},{10,0},{12,6},{14,4},{1,11},{3,9}... | collective-permute-start | bytes 786440 | tf_op jit(solution)/shard_map/ppermute | solution.py:352
  9.2 23.5 %collective-permute-start.2 = (bf16[1,2,64,1024]{3,2,1,0:T(8,128)(2,1)S(1)}, bf16[1,2,64,1024]{3,2,1,0:T(8,128)(2,1)S(1)}, u32[]{:S(2)}, u32[]{:S(2)}) collective-permute-start(bf16[1,2,64,1024]{3,2,1,0:T(8,128)(2,1)S(1)} %get-tuple-element.56), channel_id=1, source_target_pairs={{0,8},{2,10},{4,12},{6,14},{8,0},{10,2},{12,4},{14,6},{1,9},{3,11}... | collective-permute-start | bytes 786440 | tf_op jit(solution)/shard_map/ppermute | solution.py:352
  9.9 22.8 %collective-permute-start.1 = (bf16[1,2,64,1024]{3,2,1,0:T(8,128)(2,1)S(1)}, bf16[1,2,64,1024]{3,2,1,0:T(8,128)(2,1)S(1)}, u32[]{:S(2)}, u32[]{:S(2)}) collective-permute-start(bf16[1,2,64,1024]{3,2,1,0:T(8,128)(2,1)S(1)} %get-tuple-element.57), channel_id=1, source_target_pairs={{0,6},{2,4},{4,2},{6,0},{8,14},{10,12},{12,10},{14,8},{1,7},{3,5},... | collective-permute-start | bytes 786440 | tf_op jit(solution)/shard_map/ppermute | solution.py:352
  10.0 23.8 %collective-permute-start = (bf16[1,2,64,1024]{3,2,1,0:T(8,128)(2,1)S(1)}, bf16[1,2,64,1024]{3,2,1,0:T(8,128)(2,1)}, u32[]{:S(2)}, u32[]{:S(2)}) collective-permute-start(bf16[1,2,64,1024]{3,2,1,0:T(8,128)(2,1)S(1)} %get-tuple-element.54), channel_id=1, source_target_pairs={{0,4},{2,6},{4,0},{6,2},{8,12},{10,14},{12,8},{14,10},{1,5},{3,7},... | collective-permute-start | bytes 786440 | tf_op jit(solution)/shard_map/ppermute | solution.py:352
  34.9 27.1 %collective-permute-start.9 = (bf16[4,2,64,1024]{3,2,1,0:T(8,128)(2,1)S(1)}, bf16[4,2,64,1024]{3,2,1,0:T(8,128)(2,1)S(1)}, u32[]{:S(2)}, u32[]{:S(2)}) collective-permute-start(bf16[4,2,64,1024]{3,2,1,0:T(8,128)(2,1)S(1)} %pad_maximum_fusion.refs_2_), channel_id=1, source_target_pairs={{0,1},{1,0},{2,3},{3,2},{4,5},{5,4},{6,7},{7,6},{8,9},{9,8},{10,11... | collective-permute-start | bytes 3145736 | tf_op jit(solution)/shard_map/ppermute | solution.py:355
  35.5 24.9 %collective-permute-start.10 = (bf16[4,2,64,1024]{3,2,1,0:T(8,128)(2,1)S(1)}, bf16[4,2,64,1024]{3,2,1,0:T(8,128)(2,1)S(1)}, u32[]{:S(2)}, u32[]{:S(2)}) collective-permute-start(bf16[4,2,64,1024]{3,2,1,0:T(8,128)(2,1)S(1)} %pad_maximum_fusion.refs_2_), channel_id=1, source_target_pairs={{0,16},{16,0},{1,17},{17,1},{2,18},{18,2},{3,19},{19,3},{4,20},{20... | collective-permute-start | bytes 3145736 | tf_op jit(solution)/shard_map/ppermute | solution.py:355
  49.3 27.5 %collective-permute-start.8 = (bf16[4,2,64,1024]{3,2,1,0:T(8,128)(2,1)S(1)}, bf16[4,2,64,1024]{3,2,1,0:T(8,128)(2,1)S(1)}, u32[]{:S(2)}, u32[]{:S(2)}) collective-permute-start(bf16[4,2,64,1024]{3,2,1,0:T(8,128)(2,1)S(1)} %pad_maximum_fusion.1), channel_id=1, source_target_pairs={{0,2},{2,0},{4,6},{6,4},{8,10},{10,8},{12,14},{14,12},{1,3},{3,1},... | collective-permute-start | bytes 3145736 | tf_op jit(solution)/shard_map/ppermute | solution.py:352
  49.4 20.4 %collective-permute-start.4 = (bf16[1,2,64,1024]{3,2,1,0:T(8,128)(2,1)S(1)}, bf16[1,2,64,1024]{3,2,1,0:T(8,128)(2,1)S(1)}, u32[]{:S(2)}, u32[]{:S(2)}) collective-permute-start(bf16[1,2,64,1024]{3,2,1,0:T(8,128)(2,1)S(1)} %get-tuple-element.53), channel_id=1, source_target_pairs={{0,12},{2,14},{4,8},{6,10},{8,4},{10,6},{12,0},{14,2},{1,13},{3,15... | collective-permute-start | bytes 786440 | tf_op jit(solution)/shard_map/ppermute | solution.py:352
  51.2 23.5 %collective-permute-start.5 = (bf16[1,2,64,1024]{3,2,1,0:T(8,128)(2,1)S(1)}, bf16[1,2,64,1024]{3,2,1,0:T(8,128)(2,1)S(1)}, u32[]{:S(2)}, u32[]{:S(2)}) collective-permute-start(bf16[1,2,64,1024]{3,2,1,0:T(8,128)(2,1)S(1)} %get-tuple-element.52), channel_id=1, source_target_pairs={{0,14},{2,12},{4,10},{6,8},{8,6},{10,4},{12,2},{14,0},{1,15},{3,13... | collective-permute-start | bytes 786440 | tf_op jit(solution)/shard_map/ppermute | solution.py:352
  60.4 17.2 %collective-permute-start.11 = (bf16[2,2,64,1024]{3,2,1,0:T(8,128)(2,1)S(1)}, bf16[2,2,64,1024]{3,2,1,0:T(8,128)(2,1)S(1)}, u32[]{:S(2)}, u32[]{:S(2)}) collective-permute-start(bf16[2,2,64,1024]{3,2,1,0:T(8,128)(2,1)S(1)} %slice.312), channel_id=1, source_target_pairs={{0,1},{1,0},{2,3},{3,2},{4,5},{5,4},{6,7},{7,6},{8,9},{9,8},{10,11... | collective-permute-start | bytes 1572872 | tf_op jit(solution)/shard_map/ppermute | solution.py:355
  62.0 15.6 %collective-permute-start.12 = (bf16[2,2,64,1024]{3,2,1,0:T(8,128)(2,1)S(1)}, bf16[2,2,64,1024]{3,2,1,0:T(8,128)(2,1)S(1)}, u32[]{:S(2)}, u32[]{:S(2)}) collective-permute-start(bf16[2,2,64,1024]{3,2,1,0:T(8,128)(2,1)S(1)} %slice.313), channel_id=1, source_target_pairs={{0,16},{16,0},{1,17},{17,1},{2,18},{18,2},{3,19},{19,3},{4,20},{20... | collective-permute-start | bytes 1572872 | tf_op jit(solution)/shard_map/ppermute | solution.py:355
  74.7 24.8 %copy-start.4 = (bf16[2,2,64,1024]{3,2,1,0:T(8,128)(2,1)}, bf16[2,2,64,1024]{3,2,1,0:T(8,128)(2,1)S(1)}, u32[]{:S(2)}) copy-start(bf16[2,2,64,1024]{3,2,1,0:T(8,128)(2,1)S(1)} %constant_dynamic-update-slice_fusion.refs_0_) | copy-start | bytes 1572868
  74.7 24.8 %collective-permute-start.6 = (bf16[2,2,64,1024]{3,2,1,0:T(8,128)(2,1)S(1)}, bf16[2,2,64,1024]{3,2,1,0:T(8,128)(2,1)S(1)}, u32[]{:S(2)}, u32[]{:S(2)}) collective-permute-start(bf16[2,2,64,1024]{3,2,1,0:T(8,128)(2,1)S(1)} %constant_dynamic-update-slice_fusion.refs_0_), channel_id=1, source_target_pairs={{0,16},{16,0},{1,17},{17,1},{2,18},{18,2},{3,19},{19,3},{4,20},{20... | collective-permute-start | bytes 1572872 | tf_op jit(solution)/shard_map/ppermute | solution.py:355
  75.3 24.2 %collective-permute-start.7 = (bf16[2,2,64,1024]{3,2,1,0:T(8,128)(2,1)S(1)}, bf16[2,2,64,1024]{3,2,1,0:T(8,128)(2,1)S(1)}, u32[]{:S(2)}, u32[]{:S(2)}) collective-permute-start(bf16[2,2,64,1024]{3,2,1,0:T(8,128)(2,1)S(1)} %constant_dynamic-update-slice_fusion.refs_0_), channel_id=1, source_target_pairs={{0,1},{1,0},{2,3},{3,2},{4,5},{5,4},{6,7},{7,6},{8,9},{9,8},{10,11... | collective-permute-start | bytes 1572872 | tf_op jit(solution)/shard_map/ppermute | solution.py:355
  99.5 3.7 %collective-permute-start.15 = (f32[3,2,64,1024]{3,2,1,0:T(8,128)}, f32[3,2,64,1024]{3,2,1,0:T(8,128)S(1)}, u32[]{:S(2)}, u32[]{:S(2)}) collective-permute-start(f32[3,2,64,1024]{3,2,1,0:T(8,128)} %get-tuple-element.32), channel_id=1, source_target_pairs={{0,2},{2,0},{4,6},{6,4},{8,10},{10,8},{12,14},{14,12},{1,3},{3,1},... | collective-permute-start | bytes 4718600 | tf_op jit(solution)/shard_map/ppermute | solution.py:352
  99.6 8.8 %collective-permute-start.13 = (bf16[1,2,64,1024]{3,2,1,0:T(8,128)(2,1)S(1)}, bf16[1,2,64,1024]{3,2,1,0:T(8,128)(2,1)S(1)}, u32[]{:S(2)}, u32[]{:S(2)}) collective-permute-start(bf16[1,2,64,1024]{3,2,1,0:T(8,128)(2,1)S(1)} %slice.266), channel_id=1, source_target_pairs={{0,1},{1,0},{2,3},{3,2},{4,5},{5,4},{6,7},{7,6},{8,9},{9,8},{10,11... | collective-permute-start | bytes 786440 | tf_op jit(solution)/shard_map/ppermute | solution.py:355
  100.2 8.5 %collective-permute-start.14 = (bf16[1,2,64,1024]{3,2,1,0:T(8,128)(2,1)S(1)}, bf16[1,2,64,1024]{3,2,1,0:T(8,128)(2,1)S(1)}, u32[]{:S(2)}, u32[]{:S(2)}) collective-permute-start(bf16[1,2,64,1024]{3,2,1,0:T(8,128)(2,1)S(1)} %slice.267), channel_id=1, source_target_pairs={{0,16},{16,0},{1,17},{17,1},{2,18},{18,2},{3,19},{19,3},{4,20},{20... | collective-permute-start | bytes 786440 | tf_op jit(solution)/shard_map/ppermute | solution.py:355
  108.7 15.6 %collective-permute-start.16 = (s16[128,1152]{1,0:T(8,128)(2,1)S(1)}, s16[128,1152]{1,0:T(8,128)(2,1)S(1)}, u32[]{:S(2)}, u32[]{:S(2)}) collective-permute-start(s16[128,1152]{1,0:T(8,128)(2,1)S(1)} %shard_map.114), channel_id=1, source_target_pairs={{0,4},{2,6},{4,0},{6,2},{8,12},{10,14},{12,8},{14,10},{1,5},{3,7},... | collective-permute-start | bytes 884744 | tf_op jit(solution)/shard_map/ppermute | solution.py:352
  108.7 15.9 %collective-permute-start.17 = (s16[128,1152]{1,0:T(8,128)(2,1)S(1)}, s16[128,1152]{1,0:T(8,128)(2,1)S(1)}, u32[]{:S(2)}, u32[]{:S(2)}) collective-permute-start(s16[128,1152]{1,0:T(8,128)(2,1)S(1)} %shard_map.115), channel_id=1, source_target_pairs={{0,8},{2,10},{4,12},{6,14},{8,0},{10,2},{12,4},{14,6},{1,9},{3,11}... | collective-permute-start | bytes 884744 | tf_op jit(solution)/shard_map/ppermute | solution.py:352
  111.9 30.7 %copy-start.1 = (f32[3,2,64,1024]{3,2,1,0:T(8,128)S(1)}, f32[3,2,64,1024]{3,2,1,0:T(8,128)}, u32[]{:S(2)}) copy-start(f32[3,2,64,1024]{3,2,1,0:T(8,128)} %get-tuple-element.29.first_ref) | copy-start | bytes 4718596
  124.6 1.9 %collective-permute-start.18 = (f32[1,2,64,1024]{3,2,1,0:T(8,128)S(1)}, f32[1,2,64,1024]{3,2,1,0:T(8,128)S(1)}, u32[]{:S(2)}, u32[]{:S(2)}) collective-permute-start(f32[1,2,64,1024]{3,2,1,0:T(8,128)S(1)} %get-tuple-element.42), channel_id=1, source_target_pairs={{0,2},{2,0},{4,6},{6,4},{8,10},{10,8},{12,14},{14,12},{1,3},{3,1},... | collective-permute-start | bytes 1572872 | tf_op jit(solution)/shard_map/ppermute | solution.py:352
  127.1 15.4 %collective-permute-start.19 = (s16[128,1152]{1,0:T(8,128)(2,1)S(1)}, s16[128,1152]{1,0:T(8,128)(2,1)S(1)}, u32[]{:S(2)}, u32[]{:S(2)}) collective-permute-start(s16[128,1152]{1,0:T(8,128)(2,1)S(1)} %shard_map.117), channel_id=1, source_target_pairs={{0,12},{2,14},{4,8},{6,10},{8,4},{10,6},{12,0},{14,2},{1,13},{3,15... | collective-permute-start | bytes 884744 | tf_op jit(solution)/shard_map/ppermute | solution.py:352
  143.1 7.7 %collective-permute-start.20 = (f32[2,64,128]{2,1,0:T(8,128)S(1)}, f32[2,64,128]{2,1,0:T(8,128)S(1)}, u32[]{:S(2)}, u32[]{:S(2)}) collective-permute-start(f32[2,64,128]{2,1,0:T(8,128)S(1)} %get-tuple-element.44), channel_id=1, source_target_pairs={{0,1},{1,16},{16,17},{2,3},{3,18},{18,19},{4,5},{5,20},{20,21},{6,... | collective-permute-start | bytes 196616 | tf_op jit(solution)/shard_map/ppermute | solution.py:453
  147.5 7.1 %collective-permute-start.21 = (f32[2,64,128]{2,1,0:T(8,128)S(1)}, f32[2,64,128]{2,1,0:T(8,128)S(1)}, u32[]{:S(2)}, u32[]{:S(2)}) collective-permute-start(f32[2,64,128]{2,1,0:T(8,128)S(1)} %get-tuple-element.45), channel_id=1, source_target_pairs={{1,0},{16,1},{17,16},{3,2},{18,3},{19,18},{5,4},{20,5},{21,20},{7,... | collective-permute-start | bytes 196616 | tf_op jit(solution)/shard_map/ppermute | solution.py:454
  (11 other events, 101.9 us)

commit v4 on v3

--- a/solution.py
+++ b/solution.py
@@ -119,7 +119,14 @@
                 mult = gram[k, col] * res[k]
                 return tuple(acc[r - col] - mult * gram[k, r] for r in range(col, TAPS + 1))
 
-            rows_here = lax.fori_loop(0, col, reduce, rows_here)
+            def reduce_some(step, acc, reduce=reduce):
+                for n in range(4):
+                    acc = reduce(step * 4 + n, acc)
+                return acc
+
+            rows_here = lax.fori_loop(0, col // 4, reduce_some, rows_here)
+            for k in range(col // 4 * 4, col):
+                rows_here = reduce(k, rows_here)
         for r in range(col, TAPS + 1):
             gram[col, r] = rows_here[r - col]
         res[col] = 1.0 / rows_here[0]

time: 169 us -> 166 us (0.982)
  Pallas kernels: 48.1 us -> 45.7 us
    pallas_call x1, Pallas kernels: 12.4 us -> 10.1 us  [fit(): pl.pallas_call(fit_kernel, out_shape=jax.ShapeDtypeStruct(main.shape, jnp...]
where the time goes in v4:
time: 166 us
  waiting for transfers between devices  65.4 us (39%)
  Pallas kernels  45.7 us (28%)
  starting transfers between devices  25.9 us (16%)
  local copies, waits for them, and re-layouts  20.9 us (13%)
  other arithmetic  4.04 us (2%)
  between operations  3.81 us (2%)
    ppermute x12, waiting for transfers between devices, partner(): lax.ppermute(value, 'shot', [(i, i ^ step) for i in range(panel_count)])  49.8 us
    pallas_call x2, Pallas kernels, products(): pl.pallas_call(functools.partial(product_kernel, layout=tuple((len(part)...  33.4 us
    ppermute x8, waiting for transfers between devices, across(): return lax.ppermute(value, axis, [(0, 1), (1, 0)])  11.9 us
    ppermute x12, starting transfers between devices, partner(): lax.ppermute(value, 'shot', [(i, i ^ step) for i in range(panel_count)])  10.2 us
    pallas_call x1, Pallas kernels, fit(): pl.pallas_call(fit_kernel, out_shape=jax.ShapeDtypeStruct(main.shape, jnp...  10.1 us
    ppermute x8, starting transfers between devices, across(): return lax.ppermute(value, axis, [(0, 1), (1, 0)])  9.45 us
    transpose x2, local copies, waits for them, and re-layouts, turned(): return here.transpose(1, 2, 0, 3)  8.25 us
    broadcast_in_dim x25, local copies, waits for them, and re-layouts, chosen(): out = jnp.where(named[:, a, None, :, None], rows[a][None], out)  5.87 us
  transfers between devices with their start and end apart: 22, of which 13 were waited for; matrix products, arithmetic and copies ran while one was open for 9% of the time, Pallas kernels for 21%

profile of v4, /device:TPU:12, one launch (start us, length us, event | category | flops | bytes accessed | tf_op | source)
XLA Modules:
  0.0 165.8 jit_solution(16543403158564613811)
XLA Ops:
  3.4 2.1 %dynamic-slice_bitcast_fusion.4 = bf16[4,2,64,1024]{3,1,0,2:T(2,128)(2,1)S(1)} fusion(bf16[64,4,2,4096]{3,2,1,0:T(2,128)(2,1)} %param.10, s32[]{:T(128)S(6)} %select_n.75), kind=kLoop, calls=%fused_computation.7 | loop fusion | bytes 2097156 | tf_op jit(solution)/shard_map/transpose | solution.py:369
  7.1 2.1 %collective-permute-start.3 = (bf16[1,2,64,1024]{3,2,1,0:T(8,128)(2,1)S(1)}, bf16[1,2,64,1024]{3,2,1,0:T(8,128)(2,1)S(1)}, u32[]{:S(2)}, u32[]{:S(2)}) collective-permute-start(bf16[1,2,64,1024]{3,2,1,0:T(8,128)(2,1)S(1)} %get-tuple-element.55), channel_id=1, source_target_pairs={{0,10},{2,8},{4,14},{6,12},{8,2},{10,0},{12,6},{14,4},{1,11},{3,9}... | collective-permute-start | bytes 786440 | tf_op jit(solution)/shard_map/ppermute | solution.py:359
  10.0 1.6 collective-permute-start
  13.7 13.4 %collective-permute-done.3 = bf16[1,2,64,1024]{3,2,1,0:T(8,128)(2,1)S(1)} collective-permute-done((bf16[1,2,64,1024]{3,2,1,0:T(8,128)(2,1)S(1)}, bf16[1,2,64,1024]{3,2,1,0:T(8,128)(2,1)S(1)}, u32[]{:S(2)}, u32[]{:S(2)}) %collective-permute-start.3) | collective-permute-done | bytes 262176 | tf_op jit(solution)/shard_map/ppermute | solution.py:359
  27.1 5.6 %collective-permute-done.2 = bf16[1,2,64,1024]{3,2,1,0:T(8,128)(2,1)S(1)} collective-permute-done((bf16[1,2,64,1024]{3,2,1,0:T(8,128)(2,1)S(1)}, bf16[1,2,64,1024]{3,2,1,0:T(8,128)(2,1)S(1)}, u32[]{:S(2)}, u32[]{:S(2)}) %collective-permute-start.2) | collective-permute-done | bytes 262176 | tf_op jit(solution)/shard_map/ppermute | solution.py:359
  37.0 6.1 %dynamic-slice_bitcast_fusion.2 = (bf16[4,2,64,1024]{3,1,0,2:T(2,128)(2,1)S(1)}, bf16[4,2,64,1024]{3,1,0,2:T(2,128)(2,1)S(1)}, bf16[4,2,64,1024]{3,1,0,2:T(2,128)(2,1)S(1)}, bf16[4,2,64,1024]{3,1,0,2:T(2,128)(2,1)S(1)}) fusion(bf16[64,4,2,4096]{3,2,1,0:T(2,128)(2,1)} %param.10, s32[]{:T(128)S(6)} %select_n.84, s32[]{:T(128)S(6)} %select_n.94, ...), kind=kLoop, calls=%fused_computation.5 | loop fusion | bytes 8388624 | tf_op jit(solution)/shard_map/transpose | solution.py:369
  43.1 2.1 %slice_bitcast_fusion.11 = (bf16[2,64,1024]{2,0,1:T(2,128)(2,1)S(1)}, bf16[2,64,1024]{2,0,1:T(2,128)(2,1)S(1)}, bf16[2,64,1024]{2,0,1:T(2,128)(2,1)S(1)}, bf16[2...) fusion(bf16[4,2,64,1024]{3,1,0,2:T(2,128)(2,1)S(1)} %get-tuple-, ...), kind=kLoop, calls=%fused_computation.23 | loop fusion | bytes 4194304 | tf_op jit(solution)/shard_map/jit(_where)/broadcast_in_dim | solution.py:347
  46.0 2.1 %slice_bitcast_fusion.3 = (bf16[2,64,1024]{2,0,1:T(2,128)(2,1)S(1)}, bf16[2,64,1024]{2,0,1:T(2,128)(2,1)S(1)}, bf16[2,64,1024]{2,0,1:T(2,128)(2,1)S(1)}, bf16[2,...) fusion(bf16[4,2,64,1024]{3,1,0,2:T(2,128)(2,1)S(1)} %get-tuple-, ...), kind=kLoop, calls=%fused_computation.15 | loop fusion | bytes 4194304 | tf_op jit(solution)/shard_map/jit(_where)/broadcast_in_dim | solution.py:347
  49.4 1.8 %collective-permute-start.4 = (bf16[1,2,64,1024]{3,2,1,0:T(8,128)(2,1)S(1)}, bf16[1,2,64,1024]{3,2,1,0:T(8,128)(2,1)S(1)}, u32[]{:S(2)}, u32[]{:S(2)}) collective-permute-start(bf16[1,2,64,1024]{3,2,1,0:T(8,128)(2,1)S(1)} %get-tuple-element.53), channel_id=1, source_target_pairs={{0,12},{2,14},{4,8},{6,10},{8,4},{10,6},{12,0},{14,2},{1,13},{3,15... | collective-permute-start | bytes 786440 | tf_op jit(solution)/shard_map/ppermute | solution.py:359
  51.4 9.0 %collective-permute-done.10.refs_8_ = bf16[4,2,64,1024]{3,2,1,0:T(8,128)(2,1)S(1)} collective-permute-done((bf16[4,2,64,1024]{3,2,1,0:T(8,128)(2,1)S(1)}, bf16[4,2,64,1024]{3,2,1,0:T(8,128)(2,1)S(1)}, u32[]{:S(2)}, u32[]{:S(2)}) %collective-permute-start.10) | collective-permute-done | bytes 1048608 | tf_op jit(solution)/shard_map/ppermute | solution.py:362
  60.4 1.6 collective-permute-start.11
  63.6 6.2 %collective-permute-done.4 = bf16[1,2,64,1024]{3,2,1,0:T(8,128)(2,1)S(1)} collective-permute-done((bf16[1,2,64,1024]{3,2,1,0:T(8,128)(2,1)S(1)}, bf16[1,2,64,1024]{3,2,1,0:T(8,128)(2,1)S(1)}, u32[]{:S(2)}, u32[]{:S(2)}) %collective-permute-start.4) | collective-permute-done | bytes 262176 | tf_op jit(solution)/shard_map/ppermute | solution.py:359
  69.8 4.9 %collective-permute-done.5 = bf16[1,2,64,1024]{3,2,1,0:T(8,128)(2,1)S(1)} collective-permute-done((bf16[1,2,64,1024]{3,2,1,0:T(8,128)(2,1)S(1)}, bf16[1,2,64,1024]{3,2,1,0:T(8,128)(2,1)S(1)}, u32[]{:S(2)}, u32[]{:S(2)}) %collective-permute-start.5) | collective-permute-done | bytes 262176 | tf_op jit(solution)/shard_map/ppermute | solution.py:359
  78.6 20.9 %shard_map.113 = (f32[3,2,64,1024]{3,2,1,0:T(8,128)}, f32[3,2,64,1024]{3,2,1,0:T(8,128)}) custom-call(s32[4]{0:T(128)S(1)} %iota_xor_fusion.order_ref, bf16[1,2,64,1024]{3,2,1,0:T(8,128)(2,1)S(1)} %get-tuple-element.89.refs_0_, bf16[1,2,64,1024]{3,2,1,0:T(8,128)(2,1)S(1)} %get-tuple-element.61.refs_1_, bf16[4,2,64,1024]{3,2,1,0:T(8,128)(2,1)} %copy-done.5, ...), custom_call_target="tpu_custom_call" | custom-call | flops 12884901888 | bytes 16777216 | tf_op jit(solution)/shard_map/pallas_call | solution.py:244
  100.2 1.6 collective-permute-start.14
  105.8 2.6 %collective-permute-done.13.refs_3_ = bf16[1,2,64,1024]{3,2,1,0:T(8,128)(2,1)S(1)} collective-permute-done((bf16[1,2,64,1024]{3,2,1,0:T(8,128)(2,1)S(1)}, bf16[1,2,64,1024]{3,2,1,0:T(8,128)(2,1)S(1)}, u32[]{:S(2)}, u32[]{:S(2)}) %collective-permute-start.13) | collective-permute-done | bytes 262176 | tf_op jit(solution)/shard_map/ppermute | solution.py:362
  108.7 3.1 %collective-permute-start.17 = (s16[128,1152]{1,0:T(8,128)(2,1)S(1)}, s16[128,1152]{1,0:T(8,128)(2,1)S(1)}, u32[]{:S(2)}, u32[]{:S(2)}) collective-permute-start(s16[128,1152]{1,0:T(8,128)(2,1)S(1)} %shard_map.115), channel_id=1, source_target_pairs={{0,8},{2,10},{4,12},{6,14},{8,0},{10,2},{12,4},{14,6},{1,9},{3,11}... | collective-permute-start | bytes 884744 | tf_op jit(solution)/shard_map/ppermute | solution.py:359
  111.9 12.4 %shard_map.116 = (f32[1,2,64,1024]{3,2,1,0:T(8,128)S(1)}, f32[1,2,64,1024]{3,2,1,0:T(8,128)S(1)}) custom-call(s32[4]{0:T(128)S(1)} %iota_xor_fusion.order_ref, bf16[2,2,64,1024]{3,2,1,0:T(8,128)(2,1)} %copy-done.4, bf16[2,2,64,1024]{3,2,1,0:T(8,128)(2,1)} %copy-done.3, bf16[2,2,64,1024]{3,2,1,0:T(8,128)(2,1)} %copy-done.2, ...), custom_call_target="tpu_custom_call" | custom-call | flops 4294967296 | bytes 16777216 | tf_op jit(solution)/shard_map/pallas_call | solution.py:244
  124.6 1.9 %collective-permute-done.18.second_ref = f32[1,2,64,1024]{3,2,1,0:T(8,128)S(1)} collective-permute-done((f32[1,2,64,1024]{3,2,1,0:T(8,128)S(1)}, f32[1,2,64,1024]{3,2,1,0:T(8,128)S(1)}, u32[]{:S(2)}, u32[]{:S(2)}) %collective-permute-start.18) | collective-permute-done | bytes 524320 | tf_op jit(solution)/shard_map/ppermute | solution.py:359
  127.5 15.0 %collective-permute-done.19.refs_2_ = s16[128,1152]{1,0:T(8,128)(2,1)S(1)} collective-permute-done((s16[128,1152]{1,0:T(8,128)(2,1)S(1)}, s16[128,1152]{1,0:T(8,128)(2,1)S(1)}, u32[]{:S(2)}, u32[]{:S(2)}) %collective-permute-start.19) | collective-permute-done | bytes 294944 | tf_op jit(solution)/shard_map/ppermute | solution.py:359
  143.1 4.4 %collective-permute-start.20 = (f32[2,64,128]{2,1,0:T(8,128)S(1)}, f32[2,64,128]{2,1,0:T(8,128)S(1)}, u32[]{:S(2)}, u32[]{:S(2)}) collective-permute-start(f32[2,64,128]{2,1,0:T(8,128)S(1)} %get-tuple-element.44), channel_id=1, source_target_pairs={{0,1},{1,16},{16,17},{2,3},{3,18},{18,19},{4,5},{5,20},{20,21},{6,... | collective-permute-start | bytes 196616 | tf_op jit(solution)/shard_map/ppermute | solution.py:460
  147.5 1.9 %collective-permute-start.21 = (f32[2,64,128]{2,1,0:T(8,128)S(1)}, f32[2,64,128]{2,1,0:T(8,128)S(1)}, u32[]{:S(2)}, u32[]{:S(2)}) collective-permute-start(f32[2,64,128]{2,1,0:T(8,128)S(1)} %get-tuple-element.45), channel_id=1, source_target_pairs={{1,0},{16,1},{17,16},{3,2},{18,3},{19,18},{5,4},{20,5},{21,20},{7,... | collective-permute-start | bytes 196616 | tf_op jit(solution)/shard_map/ppermute | solution.py:461
  150.8 3.8 %collective-permute-done.21.high_ref = f32[2,64,128]{2,1,0:T(8,128)S(1)} collective-permute-done((f32[2,64,128]{2,1,0:T(8,128)S(1)}, f32[2,64,128]{2,1,0:T(8,128)S(1)}, u32[]{:S(2)}, u32[]{:S(2)}) %collective-permute-start.21) | collective-permute-done | bytes 65568 | tf_op jit(solution)/shard_map/ppermute | solution.py:461
  154.5 10.1 %shard_map.119 = f32[2,64,1024]{2,1,0:T(8,128)S(1)} custom-call(f32[2,64,128]{2,1,0:T(8,128)S(1)} %collective-permute-done.20.low_ref, f32[2,64,1024]{2,1,0:T(8,128)S(1)} %get-tuple-element.43.main_ref, f32[2,64,128]{2,1,0:T(8,128)S(1)} %collective-permute-done.21.high_ref, bf16[2,64,1024]{2,1,0:T(8,128)(2,1)S(1)} %bitcast.78, ...), custom_call_target="tpu_custom_call" | custom-call | tf_op jit(solution)/shard_map/pallas_call | solution.py:169
  (109 shorter events, 25.7 us)
Async XLA Ops:
  7.1 19.9 %collective-permute-start.3 = (bf16[1,2,64,1024]{3,2,1,0:T(8,128)(2,1)S(1)}, bf16[1,2,64,1024]{3,2,1,0:T(8,128)(2,1)S(1)}, u32[]{:S(2)}, u32[]{:S(2)}) collective-permute-start(bf16[1,2,64,1024]{3,2,1,0:T(8,128)(2,1)S(1)} %get-tuple-element.55), channel_id=1, source_target_pairs={{0,10},{2,8},{4,14},{6,12},{8,2},{10,0},{12,6},{14,4},{1,11},{3,9}... | collective-permute-start | bytes 786440 | tf_op jit(solution)/shard_map/ppermute | solution.py:359
  9.2 23.5 %collective-permute-start.2 = (bf16[1,2,64,1024]{3,2,1,0:T(8,128)(2,1)S(1)}, bf16[1,2,64,1024]{3,2,1,0:T(8,128)(2,1)S(1)}, u32[]{:S(2)}, u32[]{:S(2)}) collective-permute-start(bf16[1,2,64,1024]{3,2,1,0:T(8,128)(2,1)S(1)} %get-tuple-element.56), channel_id=1, source_target_pairs={{0,8},{2,10},{4,12},{6,14},{8,0},{10,2},{12,4},{14,6},{1,9},{3,11}... | collective-permute-start | bytes 786440 | tf_op jit(solution)/shard_map/ppermute | solution.py:359
  9.9 22.8 %collective-permute-start.1 = (bf16[1,2,64,1024]{3,2,1,0:T(8,128)(2,1)S(1)}, bf16[1,2,64,1024]{3,2,1,0:T(8,128)(2,1)S(1)}, u32[]{:S(2)}, u32[]{:S(2)}) collective-permute-start(bf16[1,2,64,1024]{3,2,1,0:T(8,128)(2,1)S(1)} %get-tuple-element.57), channel_id=1, source_target_pairs={{0,6},{2,4},{4,2},{6,0},{8,14},{10,12},{12,10},{14,8},{1,7},{3,5},... | collective-permute-start | bytes 786440 | tf_op jit(solution)/shard_map/ppermute | solution.py:359
  10.0 23.8 %collective-permute-start = (bf16[1,2,64,1024]{3,2,1,0:T(8,128)(2,1)S(1)}, bf16[1,2,64,1024]{3,2,1,0:T(8,128)(2,1)}, u32[]{:S(2)}, u32[]{:S(2)}) collective-permute-start(bf16[1,2,64,1024]{3,2,1,0:T(8,128)(2,1)S(1)} %get-tuple-element.54), channel_id=1, source_target_pairs={{0,4},{2,6},{4,0},{6,2},{8,12},{10,14},{12,8},{14,10},{1,5},{3,7},... | collective-permute-start | bytes 786440 | tf_op jit(solution)/shard_map/ppermute | solution.py:359
  34.9 27.1 %collective-permute-start.9 = (bf16[4,2,64,1024]{3,2,1,0:T(8,128)(2,1)S(1)}, bf16[4,2,64,1024]{3,2,1,0:T(8,128)(2,1)S(1)}, u32[]{:S(2)}, u32[]{:S(2)}) collective-permute-start(bf16[4,2,64,1024]{3,2,1,0:T(8,128)(2,1)S(1)} %pad_maximum_fusion.refs_2_), channel_id=1, source_target_pairs={{0,1},{1,0},{2,3},{3,2},{4,5},{5,4},{6,7},{7,6},{8,9},{9,8},{10,11... | collective-permute-start | bytes 3145736 | tf_op jit(solution)/shard_map/ppermute | solution.py:362
  35.5 24.9 %collective-permute-start.10 = (bf16[4,2,64,1024]{3,2,1,0:T(8,128)(2,1)S(1)}, bf16[4,2,64,1024]{3,2,1,0:T(8,128)(2,1)S(1)}, u32[]{:S(2)}, u32[]{:S(2)}) collective-permute-start(bf16[4,2,64,1024]{3,2,1,0:T(8,128)(2,1)S(1)} %pad_maximum_fusion.refs_2_), channel_id=1, source_target_pairs={{0,16},{16,0},{1,17},{17,1},{2,18},{18,2},{3,19},{19,3},{4,20},{20... | collective-permute-start | bytes 3145736 | tf_op jit(solution)/shard_map/ppermute | solution.py:362
  49.3 27.5 %collective-permute-start.8 = (bf16[4,2,64,1024]{3,2,1,0:T(8,128)(2,1)S(1)}, bf16[4,2,64,1024]{3,2,1,0:T(8,128)(2,1)S(1)}, u32[]{:S(2)}, u32[]{:S(2)}) collective-permute-start(bf16[4,2,64,1024]{3,2,1,0:T(8,128)(2,1)S(1)} %pad_maximum_fusion.1), channel_id=1, source_target_pairs={{0,2},{2,0},{4,6},{6,4},{8,10},{10,8},{12,14},{14,12},{1,3},{3,1},... | collective-permute-start | bytes 3145736 | tf_op jit(solution)/shard_map/ppermute | solution.py:359
  49.4 20.4 %collective-permute-start.4 = (bf16[1,2,64,1024]{3,2,1,0:T(8,128)(2,1)S(1)}, bf16[1,2,64,1024]{3,2,1,0:T(8,128)(2,1)S(1)}, u32[]{:S(2)}, u32[]{:S(2)}) collective-permute-start(bf16[1,2,64,1024]{3,2,1,0:T(8,128)(2,1)S(1)} %get-tuple-element.53), channel_id=1, source_target_pairs={{0,12},{2,14},{4,8},{6,10},{8,4},{10,6},{12,0},{14,2},{1,13},{3,15... | collective-permute-start | bytes 786440 | tf_op jit(solution)/shard_map/ppermute | solution.py:359
  51.2 23.5 %collective-permute-start.5 = (bf16[1,2,64,1024]{3,2,1,0:T(8,128)(2,1)S(1)}, bf16[1,2,64,1024]{3,2,1,0:T(8,128)(2,1)S(1)}, u32[]{:S(2)}, u32[]{:S(2)}) collective-permute-start(bf16[1,2,64,1024]{3,2,1,0:T(8,128)(2,1)S(1)} %get-tuple-element.52), channel_id=1, source_target_pairs={{0,14},{2,12},{4,10},{6,8},{8,6},{10,4},{12,2},{14,0},{1,15},{3,13... | collective-permute-start | bytes 786440 | tf_op jit(solution)/shard_map/ppermute | solution.py:359
  60.4 17.2 %collective-permute-start.11 = (bf16[2,2,64,1024]{3,2,1,0:T(8,128)(2,1)S(1)}, bf16[2,2,64,1024]{3,2,1,0:T(8,128)(2,1)S(1)}, u32[]{:S(2)}, u32[]{:S(2)}) collective-permute-start(bf16[2,2,64,1024]{3,2,1,0:T(8,128)(2,1)S(1)} %slice.312), channel_id=1, source_target_pairs={{0,1},{1,0},{2,3},{3,2},{4,5},{5,4},{6,7},{7,6},{8,9},{9,8},{10,11... | collective-permute-start | bytes 1572872 | tf_op jit(solution)/shard_map/ppermute | solution.py:362
  62.0 15.6 %collective-permute-start.12 = (bf16[2,2,64,1024]{3,2,1,0:T(8,128)(2,1)S(1)}, bf16[2,2,64,1024]{3,2,1,0:T(8,128)(2,1)S(1)}, u32[]{:S(2)}, u32[]{:S(2)}) collective-permute-start(bf16[2,2,64,1024]{3,2,1,0:T(8,128)(2,1)S(1)} %slice.313), channel_id=1, source_target_pairs={{0,16},{16,0},{1,17},{17,1},{2,18},{18,2},{3,19},{19,3},{4,20},{20... | collective-permute-start | bytes 1572872 | tf_op jit(solution)/shard_map/ppermute | solution.py:362
  74.7 24.8 %copy-start.4 = (bf16[2,2,64,1024]{3,2,1,0:T(8,128)(2,1)}, bf16[2,2,64,1024]{3,2,1,0:T(8,128)(2,1)S(1)}, u32[]{:S(2)}) copy-start(bf16[2,2,64,1024]{3,2,1,0:T(8,128)(2,1)S(1)} %constant_dynamic-update-slice_fusion.refs_0_) | copy-start | bytes 1572868
  74.7 24.8 %collective-permute-start.6 = (bf16[2,2,64,1024]{3,2,1,0:T(8,128)(2,1)S(1)}, bf16[2,2,64,1024]{3,2,1,0:T(8,128)(2,1)S(1)}, u32[]{:S(2)}, u32[]{:S(2)}) collective-permute-start(bf16[2,2,64,1024]{3,2,1,0:T(8,128)(2,1)S(1)} %constant_dynamic-update-slice_fusion.refs_0_), channel_id=1, source_target_pairs={{0,16},{16,0},{1,17},{17,1},{2,18},{18,2},{3,19},{19,3},{4,20},{20... | collective-permute-start | bytes 1572872 | tf_op jit(solution)/shard_map/ppermute | solution.py:362
  75.3 24.2 %collective-permute-start.7 = (bf16[2,2,64,1024]{3,2,1,0:T(8,128)(2,1)S(1)}, bf16[2,2,64,1024]{3,2,1,0:T(8,128)(2,1)S(1)}, u32[]{:S(2)}, u32[]{:S(2)}) collective-permute-start(bf16[2,2,64,1024]{3,2,1,0:T(8,128)(2,1)S(1)} %constant_dynamic-update-slice_fusion.refs_0_), channel_id=1, source_target_pairs={{0,1},{1,0},{2,3},{3,2},{4,5},{5,4},{6,7},{7,6},{8,9},{9,8},{10,11... | collective-permute-start | bytes 1572872 | tf_op jit(solution)/shard_map/ppermute | solution.py:362
  99.5 3.7 %collective-permute-start.15 = (f32[3,2,64,1024]{3,2,1,0:T(8,128)}, f32[3,2,64,1024]{3,2,1,0:T(8,128)S(1)}, u32[]{:S(2)}, u32[]{:S(2)}) collective-permute-start(f32[3,2,64,1024]{3,2,1,0:T(8,128)} %get-tuple-element.32), channel_id=1, source_target_pairs={{0,2},{2,0},{4,6},{6,4},{8,10},{10,8},{12,14},{14,12},{1,3},{3,1},... | collective-permute-start | bytes 4718600 | tf_op jit(solution)/shard_map/ppermute | solution.py:359
  99.6 8.8 %collective-permute-start.13 = (bf16[1,2,64,1024]{3,2,1,0:T(8,128)(2,1)S(1)}, bf16[1,2,64,1024]{3,2,1,0:T(8,128)(2,1)S(1)}, u32[]{:S(2)}, u32[]{:S(2)}) collective-permute-start(bf16[1,2,64,1024]{3,2,1,0:T(8,128)(2,1)S(1)} %slice.266), channel_id=1, source_target_pairs={{0,1},{1,0},{2,3},{3,2},{4,5},{5,4},{6,7},{7,6},{8,9},{9,8},{10,11... | collective-permute-start | bytes 786440 | tf_op jit(solution)/shard_map/ppermute | solution.py:362
  100.2 8.5 %collective-permute-start.14 = (bf16[1,2,64,1024]{3,2,1,0:T(8,128)(2,1)S(1)}, bf16[1,2,64,1024]{3,2,1,0:T(8,128)(2,1)S(1)}, u32[]{:S(2)}, u32[]{:S(2)}) collective-permute-start(bf16[1,2,64,1024]{3,2,1,0:T(8,128)(2,1)S(1)} %slice.267), channel_id=1, source_target_pairs={{0,16},{16,0},{1,17},{17,1},{2,18},{18,2},{3,19},{19,3},{4,20},{20... | collective-permute-start | bytes 786440 | tf_op jit(solution)/shard_map/ppermute | solution.py:362
  108.7 15.6 %collective-permute-start.16 = (s16[128,1152]{1,0:T(8,128)(2,1)S(1)}, s16[128,1152]{1,0:T(8,128)(2,1)S(1)}, u32[]{:S(2)}, u32[]{:S(2)}) collective-permute-start(s16[128,1152]{1,0:T(8,128)(2,1)S(1)} %shard_map.114), channel_id=1, source_target_pairs={{0,4},{2,6},{4,0},{6,2},{8,12},{10,14},{12,8},{14,10},{1,5},{3,7},... | collective-permute-start | bytes 884744 | tf_op jit(solution)/shard_map/ppermute | solution.py:359
  108.7 15.9 %collective-permute-start.17 = (s16[128,1152]{1,0:T(8,128)(2,1)S(1)}, s16[128,1152]{1,0:T(8,128)(2,1)S(1)}, u32[]{:S(2)}, u32[]{:S(2)}) collective-permute-start(s16[128,1152]{1,0:T(8,128)(2,1)S(1)} %shard_map.115), channel_id=1, source_target_pairs={{0,8},{2,10},{4,12},{6,14},{8,0},{10,2},{12,4},{14,6},{1,9},{3,11}... | collective-permute-start | bytes 884744 | tf_op jit(solution)/shard_map/ppermute | solution.py:359
  111.9 30.7 %copy-start.1 = (f32[3,2,64,1024]{3,2,1,0:T(8,128)S(1)}, f32[3,2,64,1024]{3,2,1,0:T(8,128)}, u32[]{:S(2)}) copy-start(f32[3,2,64,1024]{3,2,1,0:T(8,128)} %get-tuple-element.29.first_ref) | copy-start | bytes 4718596
  124.6 1.9 %collective-permute-start.18 = (f32[1,2,64,1024]{3,2,1,0:T(8,128)S(1)}, f32[1,2,64,1024]{3,2,1,0:T(8,128)S(1)}, u32[]{:S(2)}, u32[]{:S(2)}) collective-permute-start(f32[1,2,64,1024]{3,2,1,0:T(8,128)S(1)} %get-tuple-element.42), channel_id=1, source_target_pairs={{0,2},{2,0},{4,6},{6,4},{8,10},{10,8},{12,14},{14,12},{1,3},{3,1},... | collective-permute-start | bytes 1572872 | tf_op jit(solution)/shard_map/ppermute | solution.py:359
  127.1 15.4 %collective-permute-start.19 = (s16[128,1152]{1,0:T(8,128)(2,1)S(1)}, s16[128,1152]{1,0:T(8,128)(2,1)S(1)}, u32[]{:S(2)}, u32[]{:S(2)}) collective-permute-start(s16[128,1152]{1,0:T(8,128)(2,1)S(1)} %shard_map.117), channel_id=1, source_target_pairs={{0,12},{2,14},{4,8},{6,10},{8,4},{10,6},{12,0},{14,2},{1,13},{3,15... | collective-permute-start | bytes 884744 | tf_op jit(solution)/shard_map/ppermute | solution.py:359
  143.1 7.7 %collective-permute-start.20 = (f32[2,64,128]{2,1,0:T(8,128)S(1)}, f32[2,64,128]{2,1,0:T(8,128)S(1)}, u32[]{:S(2)}, u32[]{:S(2)}) collective-permute-start(f32[2,64,128]{2,1,0:T(8,128)S(1)} %get-tuple-element.44), channel_id=1, source_target_pairs={{0,1},{1,16},{16,17},{2,3},{3,18},{18,19},{4,5},{5,20},{20,21},{6,... | collective-permute-start | bytes 196616 | tf_op jit(solution)/shard_map/ppermute | solution.py:460
  147.5 7.1 %collective-permute-start.21 = (f32[2,64,128]{2,1,0:T(8,128)S(1)}, f32[2,64,128]{2,1,0:T(8,128)S(1)}, u32[]{:S(2)}, u32[]{:S(2)}) collective-permute-start(f32[2,64,128]{2,1,0:T(8,128)S(1)} %get-tuple-element.45), channel_id=1, source_target_pairs={{1,0},{16,1},{17,16},{3,2},{18,3},{19,18},{5,4},{20,5},{21,20},{7,... | collective-permute-start | bytes 196616 | tf_op jit(solution)/shard_map/ppermute | solution.py:461
  (11 other events, 101.9 us)
